TPU v7x, 32 devices: a whole 2x2x4 slice. The times are simulated.
32 devices in a mesh: pipe: 4 (over y, core), expert: 4 (over z), dp: 2 (over x).
Axes of the slice: x: 2, y: 2, z: 4, core: 2. Of those that a mesh axis runs over, the one named last changes fastest.
Arguments:
- upstream: bfloat16 [4, 1024, 2048], P('pipe', ('expert', 'dp')), may hold values from -6 to 6
- section_inputs: bfloat16 [4, 1024, 2048], P('pipe', ('expert', 'dp')), may hold values from -6 to 6
- route_ids: int32 [4, 1024, 2], P('pipe', ('expert', 'dp')), may hold values from 0 to 3, all different within a row; in each aligned block of 128 rows (0 to 127, 128 to 255, ..., all dimensions but the last counted through in order) at most 72 rows name the same one
- router_weight: bfloat16 [4, 2048, 4], P('pipe'), may hold values from -0.125 to 0.125
- w_gate: bfloat16 [4, 4, 448, 2048], P('pipe', 'expert'), may hold values from -0.125 to 0.125
- w_up: bfloat16 [4, 4, 448, 2048], P('pipe', 'expert'), may hold values from -0.125 to 0.125
- w_down: bfloat16 [4, 4, 448, 2048], P('pipe', 'expert'), may hold values from -0.25 to 0.25
- saved_preacts: bfloat16 [4, 4, 576, 896], P('pipe', 'expert', 'dp'), may hold values from -6 to 6
Outputs:
- input_grad: bfloat16 [4, 1024, 2048], P('pipe', ('expert', 'dp'))
- router_grad: float32 [4, 2048, 4], P('pipe')
Inputs may be any that keep to these rules, and one draw needn't show every extreme that they name: `route_ids`: each row names 2 different experts. Within the rows of one device no expert is named more than 72 times, and in some device's rows some expert is named exactly 72 times.
All inputs are finite; a program needn't handle non-finite values.
Results may differ from a plain program's by a relative error of at most 0.0058.
Values may be sent and summed in bfloat16 or wider, within the bound.
No kernel may reach another device: no remote copies, remote signals or barrier semaphores. Data moves between devices by JAX's collectives and lax.ppermute only.
A program may use at most 64 MiB of HBM per device.

v0:
```python
import jax
import jax.numpy as jnp
from jax import lax
from jax.sharding import PartitionSpec as P


def passed_along(value, axis, steps):
    count = lax.axis_size(axis)
    pairs = [(source, (source + steps) % count) for source in range(count)]
    return lax.ppermute(value, axis, pairs)


def swiglu_backward(received, preacts, w_gate, w_up, w_down):
    hidden_width = w_gate.shape[1]
    gate_pre = preacts[..., :hidden_width].astype(jnp.float32)
    upper = preacts[..., hidden_width:].astype(jnp.float32)
    hidden_grad = jnp.einsum("erd,efd->erf", received, w_down, preferred_element_type=jnp.float32)
    sig_gate = jax.nn.sigmoid(gate_pre)
    swish_val = gate_pre * sig_gate
    scores = jnp.sum(hidden_grad * swish_val * upper, axis=-1).astype(jnp.bfloat16)
    gate_grad = (hidden_grad * upper * sig_gate * (1.0 + gate_pre * (1.0 - sig_gate))).astype(
        jnp.bfloat16
    )
    upper_grad = (hidden_grad * swish_val).astype(jnp.bfloat16)
    rows_grad = jnp.einsum("erf,efd->erd", gate_grad, w_gate, preferred_element_type=jnp.float32)
    rows_grad = rows_grad + jnp.einsum(
        "erf,efd->erd", upper_grad, w_up, preferred_element_type=jnp.float32
    )
    return (rows_grad.astype(jnp.bfloat16), scores)


def shards(upstream, section_inputs, route_ids, router_weight, w_gate, w_up, w_down, saved_preacts):
    incoming = passed_along(upstream, "pipe", -1)[0]
    inputs = section_inputs[0]
    routes = route_ids[0]
    router = router_weight[0]
    expert_count = lax.axis_size("expert")
    replica_count = lax.axis_size("dp")
    per_device = w_gate.shape[1]
    expert_total = per_device * expert_count
    tokens = inputs.shape[0]
    feat_width = inputs.shape[1]
    top_picks = routes.shape[1]
    capacity = saved_preacts.shape[2] // expert_count
    row_count = expert_total * capacity
    pair_count = tokens * top_picks
    logits = jnp.dot(inputs, router, preferred_element_type=jnp.float32)
    onehot = (routes[:, :, None] == jnp.arange(expert_total, dtype=jnp.int32)).astype(jnp.float32)
    chosen = jnp.sum(logits[:, None, :] * onehot, axis=-1)
    first_prob = jax.nn.sigmoid(chosen[:, 0] - chosen[:, 1])
    second_prob = jax.nn.sigmoid(chosen[:, 1] - chosen[:, 0])
    gate_probs = jnp.stack([first_prob, second_prob], axis=1)
    scaled = (
        (gate_probs[:, :, None] * incoming[:, None, :])
        .astype(jnp.bfloat16)
        .reshape(pair_count, feat_width)
    )
    flat_hits = onehot.reshape(pair_count, expert_total)
    earlier = jnp.cumsum(flat_hits, axis=0) - flat_hits
    position = jnp.sum(earlier * flat_hits, axis=-1).astype(jnp.int32)
    expert_id = routes.reshape(pair_count)
    target = (expert_id % per_device * expert_count + expert_id // per_device) * capacity + position
    select = (jnp.arange(row_count, dtype=jnp.int32)[:, None] == target[None, :]).astype(
        jnp.bfloat16
    )
    outgoing = jnp.dot(select, scaled, preferred_element_type=jnp.float32).astype(jnp.bfloat16)
    outgoing = outgoing.reshape(per_device, expert_count, capacity, feat_width)
    local_pre = saved_preacts[0]
    gate_local = w_gate[0]
    up_local = w_up[0]
    down_local = w_down[0]
    received = lax.all_to_all(outgoing, "expert", split_axis=1, concat_axis=1, tiled=True)
    rows_grad, scores = swiglu_backward(
        received.reshape(per_device, expert_count * capacity, feat_width),
        local_pre,
        gate_local,
        up_local,
        down_local,
    )
    returned, returned_scores = (
        lax.all_to_all(
            rows_grad.reshape(per_device, expert_count, capacity, feat_width),
            "expert",
            split_axis=1,
            concat_axis=1,
            tiled=True,
        ),
        lax.all_to_all(
            scores.reshape(per_device, expert_count, capacity),
            "expert",
            split_axis=1,
            concat_axis=1,
            tiled=True,
        ),
    )
    returned = returned.reshape(row_count, feat_width)
    returned_scores = returned_scores.reshape(row_count)
    token_select = jnp.sum(select.reshape(row_count, tokens, top_picks), axis=2)
    mixture = lax.dot_general(
        token_select, returned, (((0,), (0,)), ((), ())), preferred_element_type=jnp.float32
    )
    choice_scores = lax.dot_general(
        select.astype(jnp.float32),
        returned_scores.astype(jnp.float32),
        (((0,), (0,)), ((), ())),
        precision=lax.Precision.HIGHEST,
    )
    pair_scores = choice_scores.reshape(tokens, top_picks)
    score_sum = jnp.sum(pair_scores, axis=1, keepdims=True)
    logit_grad = jnp.sum(
        (pair_scores - gate_probs * score_sum)[:, :, None] * onehot, axis=1
    ).astype(jnp.bfloat16)
    through_router = lax.dot_general(
        logit_grad, router, (((1,), (1,)), ((), ())), preferred_element_type=jnp.float32
    )
    result = (incoming.astype(jnp.float32) + mixture + through_router).astype(jnp.bfloat16)
    partial_grad = lax.dot_general(
        inputs, logit_grad, (((0,), (0,)), ((), ())), preferred_element_type=jnp.float32
    )
    summed = lax.psum(partial_grad, ("expert", "dp"))
    section_count = tokens * expert_count * replica_count
    return (result[None], (summed / section_count)[None])


def solution(mesh):
    in_specs = (
        P("pipe", ("expert", "dp"), None),
        P("pipe", ("expert", "dp"), None),
        P("pipe", ("expert", "dp"), None),
        P("pipe", None, None),
        P("pipe", "expert", None, None),
        P("pipe", "expert", None, None),
        P("pipe", "expert", None, None),
        P("pipe", "expert", "dp", None),
    )
    out_specs = (P("pipe", ("expert", "dp"), None), P("pipe", None, None))
    return jax.shard_map(shards, mesh=mesh, in_specs=in_specs, out_specs=out_specs, check_vma=False)
```

profile of v0, /device:TPU:0, one launch (start us, length us, event | category | flops | bytes accessed | tf_op | source)
XLA Modules:
  0.0 132.2 jit_solution(4567434136004012501)
XLA Ops:
  0.6 2.5 %collective-permute-start = (bf16[1,128,2048]{2,1,0:T(8,128)(2,1)}, bf16[1,128,2048]{2,1,0:T(8,128)(2,1)S(1)}, u32[]{:S(2)}, u32[]{:S(2)}) collective-permute-start(bf16[1,128,2048]{2,1,0:T(8,128)(2,1)} %param.8), channel_id=1, source_target_pairs={{0,24},{8,0},{16,8},{24,16},{1,25},{9,1},{17,9},{25,17},{2,26},{10... | collective-permute-start | bytes 1572872 | tf_op jit(solution)/shard_map/ppermute | solution.py:10
  3.1 0.8 copy.42
  3.9 0.1 eq.74
  4.0 0.1 eq.70
  4.2 1.2 reduce-window.6
  5.4 0.1 slice.26
  5.5 0.1 copy.45
  5.6 0.1 copy.46
  5.8 1.3 fusion.23
  7.2 0.5 copy-done.6
  7.7 0.1 copy.49
  7.9 0.1 mul.93
  8.0 0.1 add_bitcast_fusion
  8.1 2.0 %collective-permute-done = bf16[1,128,2048]{2,1,0:T(8,128)(2,1)S(1)} collective-permute-done((bf16[1,128,2048]{2,1,0:T(8,128)(2,1)}, bf16[1,128,2048]{2,1,0:T(8,128)(2,1)S(1)}, u32[]{:S(2)}, u32[]{:S(2)}) %collective-permute-start) | collective-permute-done | bytes 524320 | tf_op jit(solution)/shard_map/ppermute | solution.py:10
  10.1 0.1 bitcast_convert_fusion
  10.2 2.5 %mul.95 = f32[128,2,2048]{2,1,0:T(2,128)} broadcast(f32[128,2048]{1,0:T(8,128)S(1)} %bitcast_convert_fusion), dimensions={0,2} | broadcast | bytes 3145728 | tf_op jit(solution)/shard_map/mul | solution.py:54
  12.7 3.7 %mul.96 = f32[256,2048]{1,0:T(8,128)} reshape(f32[128,2,2048]{2,1,0:T(2,128)} %mul.95) | data formatting | bytes 4194304 | tf_op jit(solution)/shard_map/mul | solution.py:54
  16.4 3.2 %convolution_convert_fusion = bf16[288,2048]{1,0:T(8,128)(2,1)} fusion(f32[256,2048]{1,0:T(8,128)} %mul.96, f32[256]{0:T(256)S(1)} %mul.93, s32[256]{0:T(256)S(1)} %multiply_add_fusion.1), kind=kOutput, calls=%fused_computation.2 | convolution fusion | flops 303702016 | bytes 3278848 | tf_op jit(solution)/shard_map/dot_general | solution.py:66
  19.6 4.9 %all-to-all-start = ((bf16[1,4,72,2048]{3,2,0,1:T(8,128)(2,1)}), bf16[1,4,72,2048]{3,2,0,1:T(8,128)(2,1)S(1)}, u32[]{:S(2)}, u32[]{:S(2)}) async-start(bf16[1,4,72,2048]{3,2,0,1:T(8,128)(2,1)} %bitcast.9), calls=%async_computation | async-start | bytes 2359296 | tf_op jit(solution)/shard_map/all_to_all | solution.py:72
  24.5 0.7 iota_compare_fusion
  25.2 1.7 %eq.89 = pred[128,2,288]{2,1,0:T(4,128)(4,1)} reshape(pred[256,288]{1,0:T(8,128)(4,1)} %iota_compare_fusion) | data formatting | bytes 147456 | tf_op jit(solution)/shard_map/eq | solution.py:63
  26.9 0.8 convert_element_type.88
  27.7 26.2 %all-to-all-done = bf16[1,4,72,2048]{3,2,0,1:T(8,128)(2,1)S(1)} async-done(((bf16[1,4,72,2048]{3,2,0,1:T(8,128)(2,1)}), bf16[1,4,72,2048]{3,2,0,1:T(8,128)(2,1)S(1)}, u32[]{:S(2)}, u32[]{:S(2)}) %all-to-all-start) | async-done | bytes 1179680 | tf_op jit(solution)/shard_map/all_to_all | solution.py:72
  53.9 3.2 %fusion.16 = (bf16[288]{0:T(512)(128)(2,1)S(1)}, f32[1,288,448]{2,1,0:T(8,128)}) fusion(bf16[1,288,896]{2,1,0:T(8,128)(2,1)} %bitcast.86, bf16[288,2048]{1,0:T(8,128)(2,1)S(1)} %bitcast.84, bf16[1,1,448,2048]{3,2,1,0:T(8,128)(2,1)} %param.14), kind=kOutput, calls=%fused_computation.25 | convolution fusion | flops 529643232 | bytes 4047424 | tf_op jit(solution)/shard_map/erd,efd->erf/dot_general | solution.py:17
  57.2 0.7 convert_element_type.102
  57.8 3.2 %all-to-all-start.2 = ((bf16[1,4,72]{2,0,1:T(2,128)(2,1)}), bf16[1,4,72]{2,0,1:T(2,128)(2,1)S(1)}, u32[]{:S(2)}, u32[]{:S(2)}) async-start(bf16[1,4,72]{2,0,1:T(2,128)(2,1)} %convert_element_type.102), calls=%async_computation.2 | async-start | bytes 4096 | tf_op jit(solution)/shard_map/all_to_all | solution.py:88
  61.1 2.3 %fusion.5 = f32[288,2048]{1,0:T(8,128)S(1)} fusion(bf16[1,1,448,2048]{3,2,1,0:T(8,128)(2,1)S(1)} %copy-done, f32[1,288,448]{2,1,0:T(8,128)} %get-tuple-element.5, bf16[1,288,896]{2,1,0:T(8,128)(2,1)} %bitcast.87), kind=kOutput, calls=%fused_computation.10 | convolution fusion | flops 530030592 | bytes 5373952 | tf_op jit(solution)/shard_map/erf,efd->erd/dot_general | solution.py:25
  63.5 1.9 %fusion = bf16[288,2048]{1,0:T(8,128)(2,1)} fusion(f32[288,2048]{1,0:T(8,128)S(1)} %fusion.5, bf16[1,1,448,2048]{3,2,1,0:T(8,128)(2,1)S(1)} %copy-done.8, f32[1,288,448]{2,1,0:T(8,128)S(1)} %copy-done.10, bf16[1,288,896]{2,1,0:T(8,128)(2,1)S(1)} %bitcast.88), kind=kOutput, calls=%fused_computation.1 | convolution fusion | flops 530565120 | bytes 6258688 | tf_op jit(solution)/shard_map/erf,efd->erd/dot_general | solution.py:26
  65.3 1.1 all-to-all-done.2
  66.5 0.6 copy-done.5
  67.1 3.9 %all-to-all-start.1 = ((bf16[1,4,72,2048]{3,2,0,1:T(8,128)(2,1)}), bf16[1,4,72,2048]{3,2,0,1:T(8,128)(2,1)S(1)}, u32[]{:S(2)}, u32[]{:S(2)}) async-start(bf16[1,4,72,2048]{3,2,0,1:T(8,128)(2,1)} %bitcast.83), calls=%async_computation.1 | async-start | bytes 2359296 | tf_op jit(solution)/shard_map/all_to_all | solution.py:81
  71.0 1.5 %multiply_add_fusion = s32[128,2]{1,0:T(8,128)} fusion(s32[128,2]{1,0:T(8,128)} %convert_element_type.88, s32[1,128,2]{2,1,0:T(8,128)} %copy-done.1), kind=kLoop, calls=%fused_computation.47 | loop fusion | flops 512 | bytes 3072 | tf_op jit(solution)/shard_map/add | solution.py:62
  72.5 1.5 %copy.47 = s32[128,2]{0,1:T(2,128)} copy(s32[128,2]{1,0:T(8,128)} %multiply_add_fusion) | data formatting | bytes 2048 | tf_op jit(solution)/shard_map/add | solution.py:62
  74.0 1.4 %fusion.33 = bf16[288,128]{1,0:T(8,128)(2,1)} fusion(s32[128,2]{0,1:T(2,128)} %copy.47), kind=kLoop, calls=%fused_computation.45 | loop fusion | flops 184320 | bytes 74752 | tf_op jit(solution)/shard_map/reduce_sum | solution.py:98
  75.3 1.3 reduce.3
  76.6 1.3 reshape.154
  77.9 0.7 convert.3
  78.6 1.9 %fusion.25 = f32[128,2]{1,0:T(8,128)} fusion(pred[128,2,288]{2,1,0:T(4,128)(4,1)} %eq.89, f32[288]{0:T(512)S(1)} %convert.3), kind=kLoop, calls=%fused_computation.35 | loop fusion | flops 147200 | bytes 75904
  80.5 1.5 %copy.57 = f32[128,2]{0,1:T(2,128)} copy(f32[128,2]{1,0:T(8,128)} %fusion.25) | data formatting | bytes 2048 | tf_op jit(solution)/shard_map/dot_general | solution.py:102
  82.0 1.5 %reduce_sum.61 = f32[128]{0:T(128)} reduce(f32[128,2]{1,0:T(8,128)} %fusion.25, f32[]{:T(128)} %constant.37.clone.1), dimensions={1}, to_apply=%region_6.7 | reduce | flops 128 | bytes 1540 | tf_op jit(solution)/shard_map/reduce_sum | solution.py:109
  83.4 0.7 multiply_subtract_fusion
  84.1 0.7 select_reduce_fusion
  84.8 0.6 copy-done.3
  85.4 1.8 %convolution_bitcast_fusion = f32[2048,4]{0,1:T(4,128)} fusion(bf16[1,128,2048]{2,1,0:T(8,128)(2,1)} %param.9, bf16[128,4]{0,1:T(4,128)(2,1)S(1)} %select_reduce_fusion), kind=kOutput, calls=%fused_computation.7 | convolution fusion | flops 2097152 | bytes 558080 | tf_op jit(solution)/shard_map/dot_general | solution.py:117
  87.2 39.0 %psum.7 = f32[2048,4]{0,1:T(4,128)} all-reduce(f32[2048,4]{0,1:T(4,128)} %convolution_bitcast_fusion), channel_id=1, replica_groups=mesh['pipe'=4,'expert'=4,'dp'=2] {'expert','dp'}, use_global_device_ids=true, to_apply=%region_8.9 | all-reduce | flops 8192 | bytes 65536 | tf_op jit(solution)/shard_map/psum | solution.py:120
  126.2 2.1 %fusion.35 = f32[128,2048]{1,0:T(8,128)} fusion(bf16[1,2048,4]{1,2,0:T(4,128)(2,1)S(1)} %copy-done.2, bf16[128,4]{0,1:T(4,128)(2,1)} %copy-done.3), kind=kOutput, calls=%fused_computation.49 | convolution fusion | flops 2097152 | bytes 1065984 | tf_op jit(solution)/shard_map/dot_general | solution.py:113
  128.2 1.4 %multiply_bitcast_fusion = f32[1,2048,4]{1,2,0:T(4,128)} fusion(f32[2048,4]{0,1:T(4,128)} %psum.7), kind=kLoop, calls=%fused_computation.48 | loop fusion | flops 8192 | bytes 65536 | tf_op jit(solution)/shard_map/broadcast_in_dim | solution.py:122
  129.6 2.5 %fusion.3 = bf16[1,128,2048]{2,1,0:T(8,128)(2,1)} fusion(f32[128,2048]{1,0:T(8,128)} %fusion.35, bf16[288,128]{1,0:T(8,128)(2,1)} %fusion.33, bf16[288,2048]{1,0:T(8,128)(2,1)S(1)} %bitcast.81, bf16[1,128,2048]{2,1,0:T(8,128)(2,1)S(1)} %collective-permute-done), kind=kOutput, calls=%fused_computation.6 | convolution fusion | flops 152043520 | bytes 3350528 | tf_op jit(solution)/shard_map/dot_general | solution.py:99
  (30 shorter events, 0.3 us)
Async XLA Ops:
  0.6 60.4 %copy-start = (bf16[1,1,448,2048]{3,2,1,0:T(8,128)(2,1)S(1)}, bf16[1,1,448,2048]{3,2,1,0:T(8,128)(2,1)}, u32[]{:S(2)}) copy-start(bf16[1,1,448,2048]{3,2,1,0:T(8,128)(2,1)} %param.12) | copy-start | bytes 5505028
  0.6 9.5 %collective-permute-start = (bf16[1,128,2048]{2,1,0:T(8,128)(2,1)}, bf16[1,128,2048]{2,1,0:T(8,128)(2,1)S(1)}, u32[]{:S(2)}, u32[]{:S(2)}) collective-permute-start(bf16[1,128,2048]{2,1,0:T(8,128)(2,1)} %param.8), channel_id=1, source_target_pairs={{0,24},{8,0},{16,8},{24,16},{1,25},{9,1},{17,9},{25,17},{2,26},{10... | collective-permute-start | bytes 1572872 | tf_op jit(solution)/shard_map/ppermute | solution.py:10
  3.9 8.8 %copy-start.1 = (s32[1,128,2]{2,1,0:T(8,128)}, s32[1,128,2]{2,1,0:T(8,128)S(1)}, u32[]{:S(2)}) copy-start(s32[1,128,2]{2,1,0:T(8,128)S(1)} %copy.42) | copy-start | bytes 3076
  5.8 1.4 %copy-start.4 = (s32[128,2]{0,1:T(2,128)}, s32[128,2]{0,1:T(2,128)S(1)}, u32[]{:S(2)}) copy-start(s32[128,2]{0,1:T(2,128)S(1)} %copy.48) | copy-start | bytes 3076
  7.1 0.6 copy-start.6
  7.2 0.6 copy-start.7
  19.6 34.3 %all-to-all-start = ((bf16[1,4,72,2048]{3,2,0,1:T(8,128)(2,1)}), bf16[1,4,72,2048]{3,2,0,1:T(8,128)(2,1)S(1)}, u32[]{:S(2)}, u32[]{:S(2)}) async-start(bf16[1,4,72,2048]{3,2,0,1:T(8,128)(2,1)} %bitcast.9), calls=%async_computation | async-start | bytes 2359296 | tf_op jit(solution)/shard_map/all_to_all | solution.py:72
  57.8 8.7 %all-to-all-start.2 = ((bf16[1,4,72]{2,0,1:T(2,128)(2,1)}), bf16[1,4,72]{2,0,1:T(2,128)(2,1)S(1)}, u32[]{:S(2)}, u32[]{:S(2)}) async-start(bf16[1,4,72]{2,0,1:T(2,128)(2,1)} %convert_element_type.102), calls=%async_computation.2 | async-start | bytes 4096 | tf_op jit(solution)/shard_map/all_to_all | solution.py:88
  61.1 2.4 %copy-start.8 = (bf16[1,1,448,2048]{3,2,1,0:T(8,128)(2,1)S(1)}, bf16[1,1,448,2048]{3,2,1,0:T(8,128)(2,1)}, u32[]{:S(2)}) copy-start(bf16[1,1,448,2048]{3,2,1,0:T(8,128)(2,1)} %param.13) | copy-start | bytes 5505028
  61.1 2.4 %copy-start.9 = (bf16[1,1,288,896]{3,2,1,0:T(8,128)(2,1)S(1)}, bf16[1,1,288,896]{3,2,1,0:T(8,128)(2,1)}, u32[]{:S(2)}) copy-start(bf16[1,1,288,896]{3,2,1,0:T(8,128)(2,1)} %param.15) | copy-start | bytes 1548292
  61.1 2.4 %copy-start.10 = (f32[1,288,448]{2,1,0:T(8,128)S(1)}, f32[1,288,448]{2,1,0:T(8,128)}, u32[]{:S(2)}) copy-start(f32[1,288,448]{2,1,0:T(8,128)} %get-tuple-element.5) | copy-start | bytes 1548292
  66.5 0.6 copy-start.5
  66.5 59.7 %copy-start.2 = (bf16[1,2048,4]{1,2,0:T(4,128)(2,1)S(1)}, bf16[1,2048,4]{1,2,0:T(4,128)(2,1)}, u32[]{:S(2)}) copy-start(bf16[1,2048,4]{1,2,0:T(4,128)(2,1)} %param.11) | copy-start | bytes 49156
  67.1 62.6 %all-to-all-start.1 = ((bf16[1,4,72,2048]{3,2,0,1:T(8,128)(2,1)}), bf16[1,4,72,2048]{3,2,0,1:T(8,128)(2,1)S(1)}, u32[]{:S(2)}, u32[]{:S(2)}) async-start(bf16[1,4,72,2048]{3,2,0,1:T(8,128)(2,1)} %bitcast.83), calls=%async_computation.1 | async-start | bytes 2359296 | tf_op jit(solution)/shard_map/all_to_all | solution.py:81
  84.8 0.6 copy-start.3
where the time goes:
time: 133 us; the launch traced here: 132 us
  blocking collectives  39 us (29%)
  waiting for transfers between devices  29.4 us (22%)
  matrix products  18.4 us (14%)
  local copies, waits for them, and re-layouts  17 us (13%)
  starting transfers between devices  14.4 us (11%)
  other arithmetic  13.2 us (10%)
    psum x1, blocking collectives, shards(): summed = lax.psum(partial_grad, ('expert', 'dp'))  39 us
    all_to_all x1, waiting for transfers between devices, shards(): lax.all_to_all(outgoing, 'expert', split_axis=1, concat_axis=1, tiled=True)  26.2 us
    mul x3, local copies, waits for them, and re-layouts, shards(): gate_probs[:, :, None] * incoming[:, None, :]  6.34 us
    all_to_all x1, starting transfers between devices, shards(): lax.all_to_all(outgoing, 'expert', split_axis=1, concat_axis=1, tiled=True)  4.87 us
    all_to_all x1, starting transfers between devices, shards(): lax.all_to_all(rows_grad.reshape(per_device, expert_count, capacity, feat...  3.89 us
    dot_general x1, matrix products, swiglu_backward(): jnp.einsum('erd,efd->erf', received, w_down, preferred_element_type=jnp.f...  3.24 us
    all_to_all x1, starting transfers between devices, shards(): lax.all_to_all(scores.reshape(per_device, expert_count, capacity), 'exper...  3.22 us
    dot_general x1, matrix products, shards(): jnp.dot(select, scaled, preferred_element_type=jnp.float32)  3.18 us
  transfers between devices with their start and end apart: 4, of which 3 were waited for; matrix products, arithmetic and copies ran while one was open for 23% of the time, Pallas kernels for 0%

commit v1 on v0

v1 whole, which is shorter than its diff:
```python
import functools

import jax
import jax.numpy as jnp
from jax import lax
from jax.experimental import pallas as pl
from jax.experimental.pallas import tpu as pltpu
from jax.sharding import PartitionSpec as P

F32 = jnp.float32
BF16 = jnp.bfloat16
VMEM = pl.BlockSpec(memory_space=pltpu.VMEM)
SMEM = pl.BlockSpec(memory_space=pltpu.SMEM)
LANES = 128


def call(kernel, out_shape, specs, flops, size):
    return pl.pallas_call(
        kernel,
        out_shape=out_shape,
        in_specs=specs,
        out_specs=jax.tree.map(lambda _: VMEM, out_shape),
        compiler_params=pltpu.CompilerParams(vmem_limit_bytes=40 * 1024 * 1024),
        cost_estimate=pl.CostEstimate(flops=flops, bytes_accessed=size, transcendentals=0),
    )


def exchanged(value, axis, distance):
    count = lax.axis_size(axis)
    return lax.ppermute(value, axis, [(at, at ^ distance) for at in range(count)])


def route_kernel(capacity, me_ref, inputs_ref, routes_ref, router_ref, meta_ref):
    tokens = inputs_ref.shape[0]
    experts = router_ref.shape[0]
    logits = lax.dot_general(
        router_ref[...], inputs_ref[...], (((1,), (1,)), ((), ())), preferred_element_type=F32
    )
    routes = routes_ref[...]
    expert = lax.broadcasted_iota(jnp.int32, (experts, tokens), 0)
    first = (expert == routes[0:1]).astype(F32)
    second = (expert == routes[1:2]).astype(F32)
    chosen_0 = jnp.sum(logits * first, axis=0, keepdims=True)
    chosen_1 = jnp.sum(logits * second, axis=0, keepdims=True)
    earlier = lax.broadcasted_iota(jnp.int32, (tokens, tokens), 0)
    later = lax.broadcasted_iota(jnp.int32, (tokens, tokens), 1)
    before = (earlier < later).astype(BF16)
    counts = jnp.dot((first + second).astype(BF16), before, preferred_element_type=F32)
    position_0 = jnp.sum(counts * first, axis=0, keepdims=True)
    position_1 = jnp.sum(counts * second, axis=0, keepdims=True)
    away = (routes ^ me_ref[0]).astype(F32) * float(capacity)
    meta_ref[0:1] = jax.nn.sigmoid(chosen_0 - chosen_1)
    meta_ref[1:2] = jax.nn.sigmoid(chosen_1 - chosen_0)
    meta_ref[2:3] = away[0:1] + position_0
    meta_ref[3:4] = away[1:2] + position_1
    meta_ref[4:6] = routes.astype(F32)
    meta_ref[6:8] = jnp.zeros((2, tokens), F32)


def slots_of(meta, away, capacity):
    tokens = meta.shape[1]
    rows = lax.broadcasted_iota(jnp.int32, (capacity, tokens), 0).astype(F32) + float(away * capacity)
    return rows == meta[2:3], rows == meta[3:4]


def pack_kernel(aways, meta_ref, incoming_ref, *out_refs):
    meta = meta_ref[...]
    incoming = incoming_ref[...]
    for away, out_ref in zip(aways, out_refs):
        first, second = slots_of(meta, away, out_ref.shape[0])
        pick = jnp.where(first | second, 1.0, 0.0).astype(BF16)
        weight = jnp.where(first, meta[0:1], 0.0) + jnp.where(second, meta[1:2], 0.0)
        weight = jnp.sum(weight, axis=1, keepdims=True)
        rows = jnp.dot(pick, incoming, preferred_element_type=F32)
        out_ref[...] = (rows * weight).astype(BF16)


def expert_kernel(aways, me_ref, pre_ref, gate_ref, up_ref, down_ref, *refs):
    count = len(aways)
    row_refs, out_refs, score_refs = refs[:count], refs[count : 2 * count], refs[2 * count :]
    capacity, width = row_refs[0].shape[0], gate_ref.shape[0]
    me = me_ref[0]
    rows = jnp.concatenate([ref[...].astype(F32) for ref in row_refs], axis=0).astype(BF16)
    pre = jnp.concatenate([pre_ref[me ^ away].astype(F32) for away in aways], axis=0)
    hidden = lax.dot_general(
        rows, down_ref[...], (((1,), (1,)), ((), ())), preferred_element_type=F32
    )
    gate, upper = pre[:, :width], pre[:, width:]
    sig = jax.nn.sigmoid(gate)
    swish = gate * sig
    scores = jnp.sum(hidden * swish * upper, axis=1, keepdims=True).astype(BF16)
    gate_grad = (hidden * upper * sig * (1.0 + gate * (1.0 - sig))).astype(BF16)
    up_grad = (hidden * swish).astype(BF16)
    grad = jnp.dot(gate_grad, gate_ref[...], preferred_element_type=F32)
    grad = grad + jnp.dot(up_grad, up_ref[...], preferred_element_type=F32)
    spread = jnp.broadcast_to(scores.astype(F32), (count * capacity, LANES))
    for at in range(count):
        part = slice(at * capacity, (at + 1) * capacity)
        out_refs[at][...] = grad[part].astype(BF16)
        score_refs[at][...] = spread[part].astype(BF16)


def logit_kernel(aways, meta_ref, inputs_ref, *refs):
    score_refs, grad_ref, partial_ref = refs[:-2], refs[-2], refs[-1]
    meta = meta_ref[...]
    tokens = meta.shape[1]
    pair_0 = jnp.zeros((1, tokens), F32)
    pair_1 = jnp.zeros((1, tokens), F32)
    for away, ref in zip(aways, score_refs):
        first, second = slots_of(meta, away, ref.shape[0])
        score = ref[...].astype(F32)[:, 0:1]
        pair_0 = pair_0 + jnp.sum(jnp.where(first, score, 0.0), axis=0, keepdims=True)
        pair_1 = pair_1 + jnp.sum(jnp.where(second, score, 0.0), axis=0, keepdims=True)
    total = pair_0 + pair_1
    experts = grad_ref.shape[0]
    expert = lax.broadcasted_iota(jnp.int32, (experts, tokens), 0).astype(F32)
    grad = jnp.where(expert == meta[4:5], pair_0 - meta[0:1] * total, 0.0)
    grad = grad + jnp.where(expert == meta[5:6], pair_1 - meta[1:2] * total, 0.0)
    grad = grad.astype(BF16)
    grad_ref[...] = grad
    partial_ref[...] = jnp.dot(grad, inputs_ref[...], preferred_element_type=F32)


def through_kernel(incoming_ref, grad_ref, router_ref, out_ref):
    out_ref[...] = incoming_ref[...].astype(F32) + lax.dot_general(
        grad_ref[...], router_ref[...], (((0,), (0,)), ((), ())), preferred_element_type=F32
    )


def combine_kernel(aways, meta_ref, base_ref, *refs):
    out_ref = refs[-1]
    meta = meta_ref[...]
    total = base_ref[...]
    for away, ref in zip(aways, refs):
        first, second = slots_of(meta, away, ref.shape[0])
        pick = jnp.where(first | second, 1.0, 0.0).astype(BF16)
        total = total + lax.dot_general(
            pick, ref[...], (((0,), (0,)), ((), ())), preferred_element_type=F32
        )
    out_ref[...] = total.astype(out_ref.dtype)


def shards(upstream, section_inputs, route_ids, router_weight, w_gate, w_up, w_down, saved_preacts):
    sections = lax.axis_size("pipe")
    sources = lax.axis_size("expert")
    replicas = lax.axis_size("dp")
    tokens, features = section_inputs.shape[1:]
    capacity = saved_preacts.shape[2] // sources
    hidden = w_gate.shape[2]
    me = lax.axis_index("expert").astype(jnp.int32).reshape(1)
    inputs = section_inputs[0]
    routes = route_ids[0].T
    router = router_weight[0].T
    experts = router.shape[0]
    gate, up, down = w_gate[0, 0], w_up[0, 0], w_down[0, 0]
    pre = saved_preacts[0, 0].reshape(sources, capacity, 2 * hidden)
    incoming = lax.ppermute(
        upstream[0], "pipe", [(at, (at - 1) % sections) for at in range(sections)]
    )
    block = jax.ShapeDtypeStruct((capacity, features), BF16)
    spread = jax.ShapeDtypeStruct((capacity, LANES), BF16)
    block_bytes = capacity * features * 2

    meta = call(
        functools.partial(route_kernel, capacity),
        jax.ShapeDtypeStruct((8, tokens), F32),
        [SMEM, VMEM, VMEM, VMEM],
        2 * tokens * features * 8,
        tokens * features * 2,
    )(me, inputs, routes, router)

    far = [sources // 2]
    rest = [away for away in range(sources - 1, 0, -1) if away not in far]
    groups = [far + [0], rest]

    rows = {}
    for aways in (far, rest + [0]):
        packed = call(
            functools.partial(pack_kernel, aways),
            [block] * len(aways),
            [VMEM, VMEM],
            2 * tokens * features * capacity * len(aways),
            tokens * features * 2 + block_bytes * len(aways),
        )(meta, incoming)
        for away, value in zip(aways, packed):
            rows[away] = exchanged(value, "expert", away) if away else value

    back, scores = {}, {}
    for aways in groups:
        count = len(aways)
        results = call(
            functools.partial(expert_kernel, aways),
            [block] * count + [spread] * count,
            [SMEM] + [VMEM] * (4 + count),
            6 * capacity * count * features * hidden,
            3 * features * hidden * 2 + 2 * count * block_bytes,
        )(me, pre, gate, up, down, *[rows[away] for away in aways])
        for away, value, score in zip(aways, results[:count], results[count:]):
            scores[away] = exchanged(score, "expert", away) if away else score
            back[away] = exchanged(value, "expert", away) if away else value

    order = list(range(sources))
    logit_grad, partial = call(
        functools.partial(logit_kernel, order),
        [
            jax.ShapeDtypeStruct((experts, tokens), BF16),
            jax.ShapeDtypeStruct((experts, features), F32),
        ],
        [VMEM] * (2 + sources),
        2 * tokens * features * 8,
        tokens * features * 2,
    )(meta, inputs, *[scores[away] for away in order])
    step = 1
    while step < replicas:
        partial = partial + exchanged(partial, "dp", step)
        step *= 2
    if sources <= 4:
        partial = partial + sum(exchanged(partial, "expert", away) for away in range(1, sources))
    else:
        step = 1
        while step < sources:
            partial = partial + exchanged(partial, "expert", step)
            step *= 2
    router_grad = (partial / (tokens * sources * replicas)).T

    total = jax.ShapeDtypeStruct((tokens, features), F32)
    base = call(
        through_kernel, total, [VMEM] * 3, 2 * tokens * features * 8, tokens * features * 6
    )(incoming, logit_grad, router)
    early = groups[0]
    base = call(
        functools.partial(combine_kernel, early),
        total,
        [VMEM] * (2 + len(early)),
        2 * tokens * features * capacity * len(early),
        tokens * features * 8 + block_bytes * len(early),
    )(meta, base, *[back[away] for away in early])
    late = groups[1]
    result = call(
        functools.partial(combine_kernel, late),
        jax.ShapeDtypeStruct((tokens, features), BF16),
        [VMEM] * (2 + len(late)),
        2 * tokens * features * capacity * len(late),
        tokens * features * 6 + block_bytes * len(late),
    )(meta, base, *[back[away] for away in late])
    return (result[None], router_grad[None])


def solution(mesh):
    in_specs = (
        P("pipe", ("expert", "dp"), None),
        P("pipe", ("expert", "dp"), None),
        P("pipe", ("expert", "dp"), None),
        P("pipe", None, None),
        P("pipe", "expert", None, None),
        P("pipe", "expert", None, None),
        P("pipe", "expert", None, None),
        P("pipe", "expert", "dp", None),
    )
    out_specs = (P("pipe", ("expert", "dp"), None), P("pipe", None, None))
    return jax.shard_map(shards, mesh=mesh, in_specs=in_specs, out_specs=out_specs, check_vma=False)
```

time: 133 us -> 84.6 us (0.64)
  the two profiles are of different devices: /device:TPU:0 before, /device:TPU:8 now
where the time goes in v1:
time: 84.6 us; the launch traced here: 84.2 us
  waiting for transfers between devices  48 us (57%)
  starting transfers between devices  21.8 us (26%)
  Pallas kernels  6.54 us (8%)
  local copies, waits for them, and re-layouts  6.49 us (8%)
    ppermute x13, waiting for transfers between devices, exchanged(): lax.ppermute(value, axis, [(at, at ^ distance) for at in range(count)])  43.7 us
    ppermute x13, starting transfers between devices, exchanged(): lax.ppermute(value, axis, [(at, at ^ distance) for at in range(count)])  20.8 us
    unnamed x18, local copies, waits for them, and re-layouts  6.49 us
    ppermute x1, waiting for transfers between devices, shards(): lax.ppermute(upstream[0], 'pipe', [(at, (at - 1) % sections) for at in ra...  4.31 us
    pallas_call x2, Pallas kernels, shards(): call(functools.partial(expert_kernel, aways), [block] * count + [spread]...  3.31 us
  transfers between devices with their start and end apart: 14, of which 8 were waited for; matrix products, arithmetic and copies ran while one was open for 1% of the time, Pallas kernels for 6%

profile of v1, /device:TPU:8, one launch (start us, length us, event | category | flops | bytes accessed | tf_op | source)
XLA Modules:
  0.0 84.2 jit_solution(14631008317440478225)
XLA Ops:
  0.6 0.0 copy-start
  0.6 1.0 %collective-permute-start = (bf16[128,2048]{1,0:T(8,128)(2,1)}, bf16[128,2048]{1,0:T(8,128)(2,1)S(1)}, u32[]{:S(2)}, u32[]{:S(2)}) collective-permute-start(bf16[128,2048]{1,0:T(8,128)(2,1)} %bitcast.32), channel_id=1, source_target_pairs={{0,24},{8,0},{16,8},{24,16},{1,25},{9,1},{17,9},{25,17},{2,26},{10... | collective-permute-start | bytes 1572872 | tf_op jit(solution)/shard_map/ppermute | solution.py:157
  1.7 1.0 %copy-done.3 = bf16[1,128,2048]{2,1,0:T(8,128)(2,1)S(1)} copy-done((bf16[1,128,2048]{2,1,0:T(8,128)(2,1)S(1)}, bf16[1,128,2048]{2,1,0:T(8,128)(2,1)}, u32[]{:S(2)}) %copy-start.3) | copy-done | bytes 524312
  2.7 0.7 copy-done.6
  3.4 0.7 copy-done.8
  4.1 0.3 shard_map.95.meta_ref
  4.4 4.3 %collective-permute-done.incoming_ref = bf16[128,2048]{1,0:T(8,128)(2,1)S(1)} collective-permute-done((bf16[128,2048]{1,0:T(8,128)(2,1)}, bf16[128,2048]{1,0:T(8,128)(2,1)S(1)}, u32[]{:S(2)}, u32[]{:S(2)}) %collective-permute-start) | collective-permute-done | bytes 524320 | tf_op jit(solution)/shard_map/ppermute | solution.py:157
  8.7 0.2 shard_map.96
  8.9 2.7 %collective-permute-start.1 = (bf16[72,2048]{1,0:T(8,128)(2,1)S(1)}, bf16[72,2048]{1,0:T(8,128)(2,1)S(1)}, u32[]{:S(2)}, u32[]{:S(2)}) collective-permute-start(bf16[72,2048]{1,0:T(8,128)(2,1)S(1)} %shard_map.96), channel_id=1, source_target_pairs={{0,4},{2,6},{4,0},{6,2},{1,5},{3,7},{5,1},{7,3},{8,12},{10,14},{12... | collective-permute-start | bytes 884744 | tf_op jit(solution)/shard_map/ppermute | solution.py:30
  11.6 0.4 shard_map.97
  12.0 0.1 collective-permute-start.2
  12.1 1.8 %collective-permute-start.3 = (bf16[72,2048]{1,0:T(8,128)(2,1)S(1)}, bf16[72,2048]{1,0:T(8,128)(2,1)S(1)}, u32[]{:S(2)}, u32[]{:S(2)}) collective-permute-start(bf16[72,2048]{1,0:T(8,128)(2,1)S(1)} %get-tuple-element.18), channel_id=1, source_target_pairs={{0,2},{2,0},{4,6},{6,4},{1,3},{3,1},{5,7},{7,5},{8,10},{10,8},{12,... | collective-permute-start | bytes 884744 | tf_op jit(solution)/shard_map/ppermute | solution.py:30
  13.8 17.5 %collective-permute-done.1.refs_0_ = bf16[72,2048]{1,0:T(8,128)(2,1)S(1)} collective-permute-done((bf16[72,2048]{1,0:T(8,128)(2,1)S(1)}, bf16[72,2048]{1,0:T(8,128)(2,1)S(1)}, u32[]{:S(2)}, u32[]{:S(2)}) %collective-permute-start.1) | collective-permute-done | bytes 294944 | tf_op jit(solution)/shard_map/ppermute | solution.py:30
  31.3 0.0 copy-done
  31.3 1.5 %copy-done.1 = bf16[1,1,448,2048]{3,2,1,0:T(8,128)(2,1)S(1)} copy-done((bf16[1,1,448,2048]{3,2,1,0:T(8,128)(2,1)S(1)}, bf16[1,1,448,2048]{3,2,1,0:T(8,128)(2,1)}, u32[]{:S(2)}) %copy-start.1) | copy-done | bytes 1835032
  32.8 1.5 %copy-done.2 = bf16[1,1,448,2048]{3,2,1,0:T(8,128)(2,1)S(1)} copy-done((bf16[1,1,448,2048]{3,2,1,0:T(8,128)(2,1)S(1)}, bf16[1,1,448,2048]{3,2,1,0:T(8,128)(2,1)}, u32[]{:S(2)}) %copy-start.2) | copy-done | bytes 1835032
  34.3 1.0 %copy-done.5 = bf16[1,1,288,896]{3,2,1,0:T(8,128)(2,1)S(1)} copy-done((bf16[1,1,288,896]{3,2,1,0:T(8,128)(2,1)S(1)}, bf16[1,1,288,896]{3,2,1,0:T(8,128)(2,1)}, u32[]{:S(2)}) %copy-start.5) | copy-done | bytes 516120
  35.4 1.7 %shard_map.98 = (bf16[72,2048]{1,0:T(8,128)(2,1)S(1)}, bf16[72,2048]{1,0:T(8,128)(2,1)S(1)}, bf16[72,128]{1,0:T(8,128)(2,1)S(1)}, bf16[72,128]{1,0:T(8,128)(2,1)S(1)}) custom-call(s32[1]{0:T(128)} %bitcast.me_ref, bf16[4,72,896]{2,1,0:T(8,128)(2,1)S(1)} %bitcast.26, bf16[448,2048]{1,0:T(8,128)(2,1)S(1)} %bitcast.18, bf16[448,2048]{1,0:T(8,128)(2,1)S(1)} %bitcast.20, ...), custom_call_target="tpu_custom_call" | custom-call | flops 792723456 | bytes 6684672 | tf_op jit(solution)/shard_map/pallas_call | solution.py:191
  37.0 0.0 copy-start.4
  37.0 0.0 copy-start.7
  37.1 3.5 %collective-permute-start.5 = (bf16[72,128]{1,0:T(8,128)(2,1)S(1)}, bf16[72,128]{1,0:T(8,128)(2,1)S(1)}, u32[]{:S(2)}, u32[]{:S(2)}) collective-permute-start(bf16[72,128]{1,0:T(8,128)(2,1)S(1)} %get-tuple-element.20), channel_id=1, source_target_pairs={{0,4},{2,6},{4,0},{6,2},{1,5},{3,7},{5,1},{7,3},{8,12},{10,14},{12... | collective-permute-start | bytes 55304 | tf_op jit(solution)/shard_map/ppermute | solution.py:30
  40.5 0.0 collective-permute-done.2.refs_0_
  40.5 0.0 collective-permute-done.3.refs_1_
  40.5 1.7 %shard_map.99 = (bf16[72,2048]{1,0:T(8,128)(2,1)S(1)}, bf16[72,2048]{1,0:T(8,128)(2,1)S(1)}, bf16[72,128]{1,0:T(8,128)(2,1)S(1)}, bf16[72,128]{1,0:T(8,128)(2,1)S(1)}) custom-call(s32[1]{0:T(128)} %bitcast.me_ref, bf16[4,72,896]{2,1,0:T(8,128)(2,1)S(1)} %bitcast.27, bf16[448,2048]{1,0:T(8,128)(2,1)S(1)} %bitcast.19, bf16[448,2048]{1,0:T(8,128)(2,1)S(1)} %bitcast.21, ...), custom_call_target="tpu_custom_call" | custom-call | flops 792723456 | bytes 6684672 | tf_op jit(solution)/shard_map/pallas_call | solution.py:191
  42.2 0.1 collective-permute-start.4
  42.3 0.6 collective-permute-start.6
  42.9 0.0 collective-permute-done.5.refs_2_
  42.9 3.2 %collective-permute-done.4.refs_1_ = bf16[72,128]{1,0:T(8,128)(2,1)S(1)} collective-permute-done((bf16[72,128]{1,0:T(8,128)(2,1)S(1)}, bf16[72,128]{1,0:T(8,128)(2,1)S(1)}, u32[]{:S(2)}, u32[]{:S(2)}) %collective-permute-start.4) | collective-permute-done | bytes 18464 | tf_op jit(solution)/shard_map/ppermute | solution.py:30
  46.0 0.1 collective-permute-done.6.refs_3_
  46.1 0.3 shard_map.100
  46.4 1.5 %collective-permute-start.10 = (f32[4,2048]{1,0:T(4,128)S(1)}, f32[4,2048]{1,0:T(4,128)S(1)}, u32[]{:S(2)}, u32[]{:S(2)}) collective-permute-start(f32[4,2048]{1,0:T(4,128)S(1)} %get-tuple-element.27), channel_id=1, source_target_pairs={{0,1},{1,0},{2,3},{3,2},{4,5},{5,4},{6,7},{7,6},{8,9},{9,8},{10,11... | collective-permute-start | bytes 98312 | tf_op jit(solution)/shard_map/ppermute | solution.py:30
  47.9 2.4 %collective-permute-done.10 = f32[4,2048]{1,0:T(4,128)S(1)} collective-permute-done((f32[4,2048]{1,0:T(4,128)S(1)}, f32[4,2048]{1,0:T(4,128)S(1)}, u32[]{:S(2)}, u32[]{:S(2)}) %collective-permute-start.10) | collective-permute-done | bytes 32800 | tf_op jit(solution)/shard_map/ppermute | solution.py:30
  50.4 0.6 collective-permute-start.13
  51.0 5.6 %collective-permute-start.12 = (f32[4,2048]{1,0:T(4,128)S(1)}, f32[4,2048]{1,0:T(4,128)S(1)}, u32[]{:S(2)}, u32[]{:S(2)}) collective-permute-start(f32[4,2048]{1,0:T(4,128)S(1)} %add.12), channel_id=1, source_target_pairs={{0,4},{2,6},{4,0},{6,2},{1,5},{3,7},{5,1},{7,3},{8,12},{10,14},{12... | collective-permute-start | bytes 98312 | tf_op jit(solution)/shard_map/ppermute | solution.py:30
  56.5 0.0 collective-permute-start.11
  56.5 1.1 %collective-permute-start.7 = (bf16[72,2048]{1,0:T(8,128)(2,1)S(1)}, bf16[72,2048]{1,0:T(8,128)(2,1)S(1)}, u32[]{:S(2)}, u32[]{:S(2)}) collective-permute-start(bf16[72,2048]{1,0:T(8,128)(2,1)S(1)} %get-tuple-element.23), channel_id=1, source_target_pairs={{0,4},{2,6},{4,0},{6,2},{1,5},{3,7},{5,1},{7,3},{8,12},{10,14},{12... | collective-permute-start | bytes 884744 | tf_op jit(solution)/shard_map/ppermute | solution.py:30
  57.6 2.4 %collective-permute-start.8 = (bf16[72,2048]{1,0:T(8,128)(2,1)S(1)}, bf16[72,2048]{1,0:T(8,128)(2,1)S(1)}, u32[]{:S(2)}, u32[]{:S(2)}) collective-permute-start(bf16[72,2048]{1,0:T(8,128)(2,1)S(1)} %get-tuple-element.25), channel_id=1, source_target_pairs={{0,6},{2,4},{4,2},{6,0},{1,7},{3,5},{5,3},{7,1},{8,14},{10,12},{12... | collective-permute-start | bytes 884744 | tf_op jit(solution)/shard_map/ppermute | solution.py:30
  60.0 0.3 shard_map.101.base_ref
  60.3 0.0 collective-permute-done.13
  60.4 1.0 %collective-permute-start.9 = (bf16[72,2048]{1,0:T(8,128)(2,1)S(1)}, bf16[72,2048]{1,0:T(8,128)(2,1)S(1)}, u32[]{:S(2)}, u32[]{:S(2)}) collective-permute-start(bf16[72,2048]{1,0:T(8,128)(2,1)S(1)} %get-tuple-element.26), channel_id=1, source_target_pairs={{0,2},{2,0},{4,6},{6,4},{1,3},{3,1},{5,7},{7,5},{8,10},{10,8},{12,... | collective-permute-start | bytes 884744 | tf_op jit(solution)/shard_map/ppermute | solution.py:30
  61.3 4.2 %collective-permute-done.12 = f32[4,2048]{1,0:T(4,128)S(1)} collective-permute-done((f32[4,2048]{1,0:T(4,128)S(1)}, f32[4,2048]{1,0:T(4,128)S(1)}, u32[]{:S(2)}, u32[]{:S(2)}) %collective-permute-start.12) | collective-permute-done | bytes 32800 | tf_op jit(solution)/shard_map/ppermute | solution.py:30
  65.6 0.0 collective-permute-done.11
  65.6 0.6 multiply_bitcast_fusion
  66.2 9.4 %collective-permute-done.7.refs_0_ = bf16[72,2048]{1,0:T(8,128)(2,1)S(1)} collective-permute-done((bf16[72,2048]{1,0:T(8,128)(2,1)S(1)}, bf16[72,2048]{1,0:T(8,128)(2,1)S(1)}, u32[]{:S(2)}, u32[]{:S(2)}) %collective-permute-start.7) | collective-permute-done | bytes 294944 | tf_op jit(solution)/shard_map/ppermute | solution.py:30
  75.6 0.5 shard_map.102.base_ref
  76.1 6.9 %collective-permute-done.8.refs_0_ = bf16[72,2048]{1,0:T(8,128)(2,1)S(1)} collective-permute-done((bf16[72,2048]{1,0:T(8,128)(2,1)S(1)}, bf16[72,2048]{1,0:T(8,128)(2,1)S(1)}, u32[]{:S(2)}, u32[]{:S(2)}) %collective-permute-start.8) | collective-permute-done | bytes 294944 | tf_op jit(solution)/shard_map/ppermute | solution.py:30
  83.0 0.0 collective-permute-done.9.refs_1_
  83.0 1.3 %shard_map.103 = bf16[128,2048]{1,0:T(8,128)(2,1)} custom-call(f32[8,128]{1,0:T(8,128)S(1)} %shard_map.95.meta_ref, f32[128,2048]{1,0:T(8,128)S(1)} %shard_map.102.base_ref, bf16[72,2048]{1,0:T(8,128)(2,1)S(1)} %collective-permute-done.8.refs_0_, bf16[72,2048]{1,0:T(8,128)(2,1)S(1)} %collective-permute-done.9.refs_1_), custom_call_target="tpu_custom_call" | custom-call | flops 75497472 | bytes 2162688 | tf_op jit(solution)/shard_map/pallas_call | solution.py:239
  (9 shorter events, 0.0 us)
Async XLA Ops:
  0.6 30.7 %copy-start = (bf16[1,1,448,2048]{3,2,1,0:T(8,128)(2,1)S(1)}, bf16[1,1,448,2048]{3,2,1,0:T(8,128)(2,1)}, u32[]{:S(2)}) copy-start(bf16[1,1,448,2048]{3,2,1,0:T(8,128)(2,1)} %param.12) | copy-start | bytes 5505028
  0.6 8.0 %collective-permute-start = (bf16[128,2048]{1,0:T(8,128)(2,1)}, bf16[128,2048]{1,0:T(8,128)(2,1)S(1)}, u32[]{:S(2)}, u32[]{:S(2)}) collective-permute-start(bf16[128,2048]{1,0:T(8,128)(2,1)} %bitcast.32), channel_id=1, source_target_pairs={{0,24},{8,0},{16,8},{24,16},{1,25},{9,1},{17,9},{25,17},{2,26},{10... | collective-permute-start | bytes 1572872 | tf_op jit(solution)/shard_map/ppermute | solution.py:157
  1.7 1.0 %copy-start.3 = (bf16[1,128,2048]{2,1,0:T(8,128)(2,1)S(1)}, bf16[1,128,2048]{2,1,0:T(8,128)(2,1)}, u32[]{:S(2)}) copy-start(bf16[1,128,2048]{2,1,0:T(8,128)(2,1)} %param.9) | copy-start | bytes 1572868
  2.7 0.7 copy-start.6
  3.4 0.7 copy-start.8
  8.9 22.4 %collective-permute-start.1 = (bf16[72,2048]{1,0:T(8,128)(2,1)S(1)}, bf16[72,2048]{1,0:T(8,128)(2,1)S(1)}, u32[]{:S(2)}, u32[]{:S(2)}) collective-permute-start(bf16[72,2048]{1,0:T(8,128)(2,1)S(1)} %shard_map.96), channel_id=1, source_target_pairs={{0,4},{2,6},{4,0},{6,2},{1,5},{3,7},{5,1},{7,3},{8,12},{10,14},{12... | collective-permute-start | bytes 884744 | tf_op jit(solution)/shard_map/ppermute | solution.py:30
  12.0 28.6 %collective-permute-start.2 = (bf16[72,2048]{1,0:T(8,128)(2,1)S(1)}, bf16[72,2048]{1,0:T(8,128)(2,1)S(1)}, u32[]{:S(2)}, u32[]{:S(2)}) collective-permute-start(bf16[72,2048]{1,0:T(8,128)(2,1)S(1)} %get-tuple-element.17), channel_id=1, source_target_pairs={{0,6},{2,4},{4,2},{6,0},{1,7},{3,5},{5,3},{7,1},{8,14},{10,12},{12... | collective-permute-start | bytes 884744 | tf_op jit(solution)/shard_map/ppermute | solution.py:30
  12.1 28.5 %collective-permute-start.3 = (bf16[72,2048]{1,0:T(8,128)(2,1)S(1)}, bf16[72,2048]{1,0:T(8,128)(2,1)S(1)}, u32[]{:S(2)}, u32[]{:S(2)}) collective-permute-start(bf16[72,2048]{1,0:T(8,128)(2,1)S(1)} %get-tuple-element.18), channel_id=1, source_target_pairs={{0,2},{2,0},{4,6},{6,4},{1,3},{3,1},{5,7},{7,5},{8,10},{10,8},{12,... | collective-permute-start | bytes 884744 | tf_op jit(solution)/shard_map/ppermute | solution.py:30
  31.3 1.5 %copy-start.1 = (bf16[1,1,448,2048]{3,2,1,0:T(8,128)(2,1)S(1)}, bf16[1,1,448,2048]{3,2,1,0:T(8,128)(2,1)}, u32[]{:S(2)}) copy-start(bf16[1,1,448,2048]{3,2,1,0:T(8,128)(2,1)} %param.13) | copy-start | bytes 5505028
  32.8 1.5 %copy-start.2 = (bf16[1,1,448,2048]{3,2,1,0:T(8,128)(2,1)S(1)}, bf16[1,1,448,2048]{3,2,1,0:T(8,128)(2,1)}, u32[]{:S(2)}) copy-start(bf16[1,1,448,2048]{3,2,1,0:T(8,128)(2,1)} %param.14) | copy-start | bytes 5505028
  34.3 1.0 %copy-start.5 = (bf16[1,1,288,896]{3,2,1,0:T(8,128)(2,1)S(1)}, bf16[1,1,288,896]{3,2,1,0:T(8,128)(2,1)}, u32[]{:S(2)}) copy-start(bf16[1,1,288,896]{3,2,1,0:T(8,128)(2,1)} %param.15) | copy-start | bytes 1548292
  37.0 9.1 %copy-start.4 = (bf16[1,128,2048]{2,1,0:T(8,128)(2,1)S(1)}, bf16[1,128,2048]{2,1,0:T(8,128)(2,1)}, u32[]{:S(2)}) copy-start(bf16[1,128,2048]{2,1,0:T(8,128)(2,1)} %param.9) | copy-start | bytes 1572868
  37.0 23.0 %copy-start.7 = (bf16[1,2048,4]{1,2,0:T(4,128)(2,1)S(1)}, bf16[1,2048,4]{1,2,0:T(4,128)(2,1)}, u32[]{:S(2)}) copy-start(bf16[1,2048,4]{1,2,0:T(4,128)(2,1)} %param.11) | copy-start | bytes 49156
  37.1 5.8 %collective-permute-start.5 = (bf16[72,128]{1,0:T(8,128)(2,1)S(1)}, bf16[72,128]{1,0:T(8,128)(2,1)S(1)}, u32[]{:S(2)}, u32[]{:S(2)}) collective-permute-start(bf16[72,128]{1,0:T(8,128)(2,1)S(1)} %get-tuple-element.20), channel_id=1, source_target_pairs={{0,4},{2,6},{4,0},{6,2},{1,5},{3,7},{5,1},{7,3},{8,12},{10,14},{12... | collective-permute-start | bytes 55304 | tf_op jit(solution)/shard_map/ppermute | solution.py:30
  42.2 3.8 %collective-permute-start.4 = (bf16[72,128]{1,0:T(8,128)(2,1)S(1)}, bf16[72,128]{1,0:T(8,128)(2,1)S(1)}, u32[]{:S(2)}, u32[]{:S(2)}) collective-permute-start(bf16[72,128]{1,0:T(8,128)(2,1)S(1)} %get-tuple-element.19), channel_id=1, source_target_pairs={{0,2},{2,0},{4,6},{6,4},{1,3},{3,1},{5,7},{7,5},{8,10},{10,8},{12,... | collective-permute-start | bytes 55304 | tf_op jit(solution)/shard_map/ppermute | solution.py:30
  42.3 3.8 %collective-permute-start.6 = (bf16[72,128]{1,0:T(8,128)(2,1)S(1)}, bf16[72,128]{1,0:T(8,128)(2,1)S(1)}, u32[]{:S(2)}, u32[]{:S(2)}) collective-permute-start(bf16[72,128]{1,0:T(8,128)(2,1)S(1)} %get-tuple-element.21), channel_id=1, source_target_pairs={{0,6},{2,4},{4,2},{6,0},{1,7},{3,5},{5,3},{7,1},{8,14},{10,12},{12... | collective-permute-start | bytes 55304 | tf_op jit(solution)/shard_map/ppermute | solution.py:30
  46.4 4.0 %collective-permute-start.10 = (f32[4,2048]{1,0:T(4,128)S(1)}, f32[4,2048]{1,0:T(4,128)S(1)}, u32[]{:S(2)}, u32[]{:S(2)}) collective-permute-start(f32[4,2048]{1,0:T(4,128)S(1)} %get-tuple-element.27), channel_id=1, source_target_pairs={{0,1},{1,0},{2,3},{3,2},{4,5},{5,4},{6,7},{7,6},{8,9},{9,8},{10,11... | collective-permute-start | bytes 98312 | tf_op jit(solution)/shard_map/ppermute | solution.py:30
  50.4 10.0 %collective-permute-start.13 = (f32[4,2048]{1,0:T(4,128)S(1)}, f32[4,2048]{1,0:T(4,128)S(1)}, u32[]{:S(2)}, u32[]{:S(2)}) collective-permute-start(f32[4,2048]{1,0:T(4,128)S(1)} %add.12), channel_id=1, source_target_pairs={{0,6},{2,4},{4,2},{6,0},{1,7},{3,5},{5,3},{7,1},{8,14},{10,12},{12... | collective-permute-start | bytes 98312 | tf_op jit(solution)/shard_map/ppermute | solution.py:30
  51.0 14.6 %collective-permute-start.12 = (f32[4,2048]{1,0:T(4,128)S(1)}, f32[4,2048]{1,0:T(4,128)S(1)}, u32[]{:S(2)}, u32[]{:S(2)}) collective-permute-start(f32[4,2048]{1,0:T(4,128)S(1)} %add.12), channel_id=1, source_target_pairs={{0,4},{2,6},{4,0},{6,2},{1,5},{3,7},{5,1},{7,3},{8,12},{10,14},{12... | collective-permute-start | bytes 98312 | tf_op jit(solution)/shard_map/ppermute | solution.py:30
  56.5 9.0 %collective-permute-start.11 = (f32[4,2048]{1,0:T(4,128)S(1)}, f32[4,2048]{1,0:T(4,128)S(1)}, u32[]{:S(2)}, u32[]{:S(2)}) collective-permute-start(f32[4,2048]{1,0:T(4,128)S(1)} %add.12), channel_id=1, source_target_pairs={{0,2},{2,0},{4,6},{6,4},{1,3},{3,1},{5,7},{7,5},{8,10},{10,8},{12,... | collective-permute-start | bytes 98312 | tf_op jit(solution)/shard_map/ppermute | solution.py:30
  56.5 19.1 %collective-permute-start.7 = (bf16[72,2048]{1,0:T(8,128)(2,1)S(1)}, bf16[72,2048]{1,0:T(8,128)(2,1)S(1)}, u32[]{:S(2)}, u32[]{:S(2)}) collective-permute-start(bf16[72,2048]{1,0:T(8,128)(2,1)S(1)} %get-tuple-element.23), channel_id=1, source_target_pairs={{0,4},{2,6},{4,0},{6,2},{1,5},{3,7},{5,1},{7,3},{8,12},{10,14},{12... | collective-permute-start | bytes 884744 | tf_op jit(solution)/shard_map/ppermute | solution.py:30
  57.6 25.4 %collective-permute-start.8 = (bf16[72,2048]{1,0:T(8,128)(2,1)S(1)}, bf16[72,2048]{1,0:T(8,128)(2,1)S(1)}, u32[]{:S(2)}, u32[]{:S(2)}) collective-permute-start(bf16[72,2048]{1,0:T(8,128)(2,1)S(1)} %get-tuple-element.25), channel_id=1, source_target_pairs={{0,6},{2,4},{4,2},{6,0},{1,7},{3,5},{5,3},{7,1},{8,14},{10,12},{12... | collective-permute-start | bytes 884744 | tf_op jit(solution)/shard_map/ppermute | solution.py:30
  60.4 22.6 %collective-permute-start.9 = (bf16[72,2048]{1,0:T(8,128)(2,1)S(1)}, bf16[72,2048]{1,0:T(8,128)(2,1)S(1)}, u32[]{:S(2)}, u32[]{:S(2)}) collective-permute-start(bf16[72,2048]{1,0:T(8,128)(2,1)S(1)} %get-tuple-element.26), channel_id=1, source_target_pairs={{0,2},{2,0},{4,6},{6,4},{1,3},{3,1},{5,7},{7,5},{8,10},{10,8},{12,... | collective-permute-start | bytes 884744 | tf_op jit(solution)/shard_map/ppermute | solution.py:30

commit v2 on v1

v2 whole, which is shorter than its diff:
```python
import functools

import jax
import jax.numpy as jnp
from jax import lax
from jax.experimental import pallas as pl
from jax.experimental.pallas import tpu as pltpu
from jax.sharding import PartitionSpec as P

F32 = jnp.float32
BF16 = jnp.bfloat16
VMEM = pl.BlockSpec(memory_space=pltpu.VMEM)
ANY = pl.BlockSpec(memory_space=pl.ANY)
SMEM = pl.BlockSpec(memory_space=pltpu.SMEM)
LANES = 128


def call(kernel, out_shape, specs, flops, size):
    return pl.pallas_call(
        kernel,
        out_shape=out_shape,
        in_specs=specs,
        out_specs=jax.tree.map(lambda _: VMEM, out_shape),
        compiler_params=pltpu.CompilerParams(vmem_limit_bytes=40 * 1024 * 1024),
        cost_estimate=pl.CostEstimate(flops=flops, bytes_accessed=size, transcendentals=0),
    )


def exchanged(value, axis, distance):
    count = lax.axis_size(axis)
    return lax.ppermute(value, axis, [(at, at ^ distance) for at in range(count)])


def route_kernel(capacity, me_ref, inputs_ref, routes_ref, router_ref, meta_ref):
    tokens = inputs_ref.shape[0]
    experts = router_ref.shape[0]
    logits = lax.dot_general(
        router_ref[...], inputs_ref[...], (((1,), (1,)), ((), ())), preferred_element_type=F32
    )
    routes = routes_ref[...]
    expert = lax.broadcasted_iota(jnp.int32, (experts, tokens), 0)
    first = (expert == routes[0:1]).astype(F32)
    second = (expert == routes[1:2]).astype(F32)
    chosen_0 = jnp.sum(logits * first, axis=0, keepdims=True)
    chosen_1 = jnp.sum(logits * second, axis=0, keepdims=True)
    earlier = lax.broadcasted_iota(jnp.int32, (tokens, tokens), 0)
    later = lax.broadcasted_iota(jnp.int32, (tokens, tokens), 1)
    before = (earlier < later).astype(BF16)
    counts = jnp.dot((first + second).astype(BF16), before, preferred_element_type=F32)
    position_0 = jnp.sum(counts * first, axis=0, keepdims=True)
    position_1 = jnp.sum(counts * second, axis=0, keepdims=True)
    away = (routes ^ me_ref[0]).astype(F32) * float(capacity)
    meta_ref[0:1] = jax.nn.sigmoid(chosen_0 - chosen_1)
    meta_ref[1:2] = jax.nn.sigmoid(chosen_1 - chosen_0)
    meta_ref[2:3] = away[0:1] + position_0
    meta_ref[3:4] = away[1:2] + position_1
    meta_ref[4:6] = routes.astype(F32)
    meta_ref[6:8] = jnp.zeros((2, tokens), F32)


def slots_of(meta, away, capacity):
    tokens = meta.shape[1]
    rows = lax.broadcasted_iota(jnp.int32, (capacity, tokens), 0).astype(F32) + float(away * capacity)
    return rows == meta[2:3], rows == meta[3:4]


def packed_rows(meta, values, away, capacity):
    first, second = slots_of(meta, away, capacity)
    pick = jnp.where(first | second, 1.0, 0.0).astype(BF16)
    weight = jnp.where(first, meta[0:1], 0.0) + jnp.where(second, meta[1:2], 0.0)
    weight = jnp.sum(weight, axis=1, keepdims=True)
    rows = jnp.dot(pick, values, preferred_element_type=F32)
    return (rows * weight).astype(BF16)


def pack_kernel(whole, part, meta_ref, incoming_ref, *out_refs):
    meta = meta_ref[...]
    incoming = incoming_ref[...]
    for away, out_ref in zip(list(whole) + list(part), out_refs):
        capacity, width = out_ref.shape
        out_ref[...] = packed_rows(meta, incoming[:, incoming.shape[1] - width :], away, capacity)


def held_kernel(*refs):
    refs[-1][...] = refs[0][...]


def after_kernel(aways, _raw, _held, meta_ref, incoming_ref, *out_refs):
    pack_kernel([], aways, meta_ref, incoming_ref, *out_refs)


def relay_kernel(aways, _held, meta_ref, raw_ref, *out_refs):
    pack_kernel([], aways, meta_ref, raw_ref, *out_refs)


def swiglu_grads(rows, pre, gate_ref, up_ref, down_ref):
    width = gate_ref.shape[0]
    hidden = lax.dot_general(
        rows, down_ref[...], (((1,), (1,)), ((), ())), preferred_element_type=F32
    )
    gate, upper = pre[:, :width], pre[:, width:]
    sig = jax.nn.sigmoid(gate)
    swish = gate * sig
    scores = jnp.sum(hidden * swish * upper, axis=1, keepdims=True).astype(BF16)
    gate_grad = (hidden * upper * sig * (1.0 + gate * (1.0 - sig))).astype(BF16)
    up_grad = (hidden * swish).astype(BF16)
    grad = jnp.dot(gate_grad, gate_ref[...], preferred_element_type=F32)
    grad = grad + jnp.dot(up_grad, up_ref[...], preferred_element_type=F32)
    return grad, jnp.broadcast_to(scores.astype(F32), (rows.shape[0], LANES))


def first_kernel(
    aways, me_ref, pre_ref, gate_ref, up_ref, down_ref, meta_ref, raw_ref, tail_ref, *refs
):
    count = len(aways)
    row_refs, out_refs = refs[: count - 1], refs[count - 1 :]
    capacity = tail_ref.shape[0]
    me = me_ref[0]
    head = packed_rows(meta_ref[...], raw_ref[...], aways[-1], capacity).astype(F32)
    far = jnp.concatenate([head, tail_ref[...].astype(F32)], axis=1)
    rows = jnp.concatenate([ref[...].astype(F32) for ref in row_refs] + [far], axis=0).astype(BF16)
    pre = jnp.concatenate([pre_ref[me ^ away].astype(F32) for away in aways], axis=0)
    grad, spread = swiglu_grads(rows, pre, gate_ref, up_ref, down_ref)
    features = grad.shape[1]
    for at in range(count):
        part = slice(at * capacity, (at + 1) * capacity)
        out_refs[at][:, :features] = grad[part].astype(BF16)
        out_refs[at][:, features:] = spread[part].astype(BF16)


def last_kernel(aways, early, me_ref, pre_ref, gate_ref, up_ref, down_ref, _, *refs):
    count = len(aways)
    head_refs, tail_refs, out_refs = refs[:count], refs[count : 2 * count], refs[2 * count :]
    capacity = head_refs[0].shape[0]
    me = me_ref[0]
    rows = [
        jnp.concatenate([head[...].astype(F32), tail[...].astype(F32)], axis=1)
        for head, tail in zip(head_refs, tail_refs)
    ]
    rows = jnp.concatenate(rows, axis=0).astype(BF16)
    pre = jnp.concatenate([pre_ref[me ^ away].astype(F32) for away in aways], axis=0)
    grad, spread = swiglu_grads(rows, pre, gate_ref, up_ref, down_ref)
    for at in range(count):
        part = slice(at * capacity, (at + 1) * capacity)
        out_refs[at][:, :early] = grad[part, :early].astype(BF16)
        out_refs[at][:, early:] = spread[part].astype(BF16)
        out_refs[count + at][...] = grad[part, early:].astype(BF16)


def mixed_rows(meta, aways, refs, width):
    total = 0.0
    for away, ref in zip(aways, refs):
        first, second = slots_of(meta, away, ref.shape[0])
        pick = jnp.where(first | second, 1.0, 0.0).astype(BF16)
        total = total + lax.dot_general(
            pick, ref[:, :width], (((0,), (0,)), ((), ())), preferred_element_type=F32
        )
    return total


def logit_kernel(whole, last, meta_ref, inputs_ref, incoming_ref, router_ref, *refs):
    whole_refs, last_refs = refs[: len(whole)], refs[len(whole) : -2]
    partial_ref, base_ref = refs[-2], refs[-1]
    meta = meta_ref[...]
    tokens, features = incoming_ref.shape
    pair_0 = jnp.zeros((1, tokens), F32)
    pair_1 = jnp.zeros((1, tokens), F32)
    for away, ref in zip(list(whole) + list(last), refs[:-2]):
        capacity, width = ref.shape
        first, second = slots_of(meta, away, capacity)
        score = ref[:, width - LANES :].astype(F32)[:, 0:1]
        pair_0 = pair_0 + jnp.sum(jnp.where(first, score, 0.0), axis=0, keepdims=True)
        pair_1 = pair_1 + jnp.sum(jnp.where(second, score, 0.0), axis=0, keepdims=True)
    total = pair_0 + pair_1
    experts = router_ref.shape[0]
    expert = lax.broadcasted_iota(jnp.int32, (experts, tokens), 0).astype(F32)
    grad = jnp.where(expert == meta[4:5], pair_0 - meta[0:1] * total, 0.0)
    grad = grad + jnp.where(expert == meta[5:6], pair_1 - meta[1:2] * total, 0.0)
    grad = grad.astype(BF16)
    partial_ref[...] = jnp.dot(grad, inputs_ref[...], preferred_element_type=F32)
    through = lax.dot_general(
        grad, router_ref[...], (((0,), (0,)), ((), ())), preferred_element_type=F32
    )
    base = incoming_ref[...].astype(F32) + through + mixed_rows(meta, whole, whole_refs, features)
    split = last_refs[0].shape[1] - LANES
    base_ref[:, :split] = base[:, :split] + mixed_rows(meta, last, last_refs, split)
    base_ref[:, split:] = base[:, split:]


def final_kernel(aways, count, meta_ref, base_ref, *refs):
    out_ref, router_ref = refs[-2], refs[-1]
    width = refs[0].shape[1]
    split = out_ref.shape[1] - width
    out_ref[:, :split] = base_ref[:, :split].astype(out_ref.dtype)
    total = base_ref[:, split:] + mixed_rows(meta_ref[...], aways, refs[: len(aways)], width)
    out_ref[:, split:] = total.astype(out_ref.dtype)
    parts = [ref[...].astype(F32) for ref in refs[len(aways) : -2]]
    router_ref[...] = sum(parts[1:], parts[0]) / float(count)


def shards(upstream, section_inputs, route_ids, router_weight, w_gate, w_up, w_down, saved_preacts):
    sections = lax.axis_size("pipe")
    sources = lax.axis_size("expert")
    replicas = lax.axis_size("dp")
    tokens, features = section_inputs.shape[1:]
    capacity = saved_preacts.shape[2] // sources
    hidden = w_gate.shape[2]
    me = lax.axis_index("expert").astype(jnp.int32).reshape(1)
    inputs = section_inputs[0]
    routes = route_ids[0].T
    router = router_weight[0].T
    experts = router.shape[0]
    gate, up, down = w_gate[0, 0], w_up[0, 0], w_down[0, 0]
    pre = saved_preacts[0, 0].reshape(sources, capacity, 2 * hidden)
    half = sources // 2
    split = features * 5 // 8
    early = features * 11 // 16
    near, last = list(range(half)), list(range(half + 1, sources))

    def shape(rows, columns, kind=BF16):
        return jax.ShapeDtypeStruct((rows, columns), kind)

    block_bytes = capacity * features * 2
    weight_bytes = 3 * features * hidden * 2
    row_flops = 6 * capacity * features * hidden
    pick_flops = 2 * tokens * features * capacity

    earlier_section = [(at, (at - 1) % sections) for at in range(sections)]
    raw = lax.ppermute(
        upstream[0, :, :split],
        ("pipe", "expert"),
        [
            (source * sources + at, target * sources + (at ^ half))
            for source, target in earlier_section
            for at in range(sources)
        ],
    )
    incoming = lax.ppermute(upstream[0], "pipe", earlier_section)
    meta = call(
        functools.partial(route_kernel, capacity),
        shape(8, tokens, F32),
        [SMEM, VMEM, VMEM, VMEM],
        2 * tokens * features * 8,
        tokens * features * 2,
    )(me, inputs, routes, router)
    far_meta = exchanged(meta, "expert", half)

    packed = call(
        functools.partial(pack_kernel, near, [half]),
        [shape(capacity, features)] * half + [shape(capacity, features - split)],
        [VMEM, VMEM],
        pick_flops * (half + 1),
        tokens * features * 2 + block_bytes * (half + 1),
    )(meta, incoming)
    far_tail = exchanged(packed[half], "expert", half)
    rows = [exchanged(packed[away], "expert", away) if away else packed[0] for away in near]

    held = call(
        held_kernel, shape(8, tokens, F32), [VMEM] * 5 + [ANY], 0, 0
    )(meta, pre, gate, up, down, packed[0])
    late = call(
        functools.partial(after_kernel, last),
        [shape(capacity, features - split)] * len(last),
        [ANY] * 2 + [VMEM] * 2,
        pick_flops * len(last),
        tokens * features * 2 + block_bytes * len(last),
    )(raw, held, meta, incoming)
    relays = call(
        functools.partial(relay_kernel, last),
        [shape(capacity, split)] * len(last),
        [ANY] + [VMEM] * 2,
        pick_flops * len(last),
        tokens * features * 2 + block_bytes * len(last),
    )(held, far_meta, raw)
    tails = [exchanged(value, "expert", away) for away, value in zip(last, late)]
    heads = [exchanged(value, "expert", away - half) for away, value in zip(last, relays)]

    whole = near + [half]
    first = call(
        functools.partial(first_kernel, whole),
        [shape(capacity, features + LANES)] * len(whole),
        [SMEM] + [VMEM] * (7 + half),
        row_flops * len(whole),
        weight_bytes + 2 * block_bytes * len(whole),
    )(me, pre, gate, up, down, far_meta, raw, far_tail, *rows)
    back = [exchanged(value, "expert", away) if away else value for away, value in zip(whole, first)]

    ends = call(
        functools.partial(last_kernel, last, early),
        [shape(capacity, early + LANES)] * len(last) + [shape(capacity, features - early)] * len(last),
        [SMEM] + [VMEM] * 4 + [ANY] + [VMEM] * (2 * len(last)),
        row_flops * len(last),
        weight_bytes + 2 * block_bytes * len(last),
    )(me, pre, gate, up, down, first[0], *heads, *tails)
    back_heads = [exchanged(value, "expert", away) for away, value in zip(last, ends)]
    back_tails = [exchanged(value, "expert", away) for away, value in zip(last, ends[len(last) :])]

    partial, base = call(
        functools.partial(logit_kernel, whole, last),
        [shape(experts, features, F32), shape(tokens, features, F32)],
        [VMEM] * (4 + sources),
        pick_flops * sources,
        tokens * features * 8 + block_bytes * sources,
    )(meta, inputs, incoming, router, *back, *back_heads)
    step = 1
    while step < replicas:
        partial = partial + exchanged(partial, "dp", step)
        step *= 2
    step = 1
    while step < sources // 4:
        partial = partial + exchanged(partial, "expert", step)
        step *= 2
    sent = partial.astype(BF16)
    parts = [partial] + [exchanged(sent, "expert", away) for away in range(step, sources, step)]

    result, router_grad = call(
        functools.partial(final_kernel, last, tokens * sources * replicas),
        [shape(tokens, features), shape(experts, features, F32)],
        [VMEM] * (2 + len(last) + len(parts)),
        pick_flops * len(last),
        tokens * features * 6 + block_bytes * len(last),
    )(meta, base, *back_tails, *parts)
    return (result[None], router_grad.T[None])


def solution(mesh):
    in_specs = (
        P("pipe", ("expert", "dp"), None),
        P("pipe", ("expert", "dp"), None),
        P("pipe", ("expert", "dp"), None),
        P("pipe", None, None),
        P("pipe", "expert", None, None),
        P("pipe", "expert", None, None),
        P("pipe", "expert", None, None),
        P("pipe", "expert", "dp", None),
    )
    out_specs = (P("pipe", ("expert", "dp"), None), P("pipe", None, None))
    return jax.shard_map(shards, mesh=mesh, in_specs=in_specs, out_specs=out_specs, check_vma=False)
```

time: 84.6 us -> 73.3 us (0.87)
  the two profiles are of different devices: /device:TPU:8 before, /device:TPU:0 now
where the time goes in v2:
time: 73.3 us; the launch traced here: 72.9 us
  starting transfers between devices  37.5 us (51%)
  waiting for transfers between devices  20.2 us (28%)
  local copies, waits for them, and re-layouts  7.99 us (11%)
  Pallas kernels  6.49 us (9%)
  between operations  0.76 us (1%)
    ppermute x13, starting transfers between devices, exchanged(): lax.ppermute(value, axis, [(at, at ^ distance) for at in range(count)])  32.3 us
    ppermute x13, waiting for transfers between devices, exchanged(): lax.ppermute(value, axis, [(at, at ^ distance) for at in range(count)])  19.3 us
    unnamed x24, local copies, waits for them, and re-layouts  6.97 us
    ppermute x1, starting transfers between devices, shards(): lax.ppermute(upstream[0, :, :split], ('pipe', 'expert'), [(source * sourc...  2.72 us
    ppermute x1, starting transfers between devices, shards(): incoming = lax.ppermute(upstream[0], 'pipe', earlier_section)  2.46 us
    pallas_call x1, Pallas kernels, shards(): call(functools.partial(first_kernel, whole), [shape(capacity, features +...  1.97 us
    pallas_call x1, Pallas kernels, shards(): call(functools.partial(last_kernel, last, early), [shape(capacity, early...  1.55 us
  transfers between devices with their start and end apart: 15, of which 8 were waited for; matrix products, arithmetic and copies ran while one was open for 1% of the time, Pallas kernels for 6%

profile of v2, /device:TPU:0, one launch (start us, length us, event | category | flops | bytes accessed | tf_op | source)
XLA Modules:
  0.0 72.9 jit_solution(5456125197304976006)
XLA Ops:
  0.6 2.5 %collective-permute-start = (bf16[128,2048]{1,0:T(8,128)(2,1)}, bf16[128,2048]{1,0:T(8,128)(2,1)S(1)}, u32[]{:S(2)}, u32[]{:S(2)}) collective-permute-start(bf16[128,2048]{1,0:T(8,128)(2,1)} %bitcast.36), channel_id=1, source_target_pairs={{0,24},{8,0},{16,8},{24,16},{1,25},{9,1},{17,9},{25,17},{2,26},{10... | collective-permute-start | bytes 1572872 | tf_op jit(solution)/shard_map/ppermute | solution.py:238
  3.1 1.0 %slice_bitcast_fusion = bf16[128,1280]{1,0:T(8,128)(2,1)S(1)} fusion(bf16[1,128,2048]{2,1,0:T(8,128)(2,1)} %param.8), kind=kLoop, calls=%fused_computation | loop fusion | bytes 655360 | tf_op jit(solution)/shard_map/squeeze | solution.py:230
  4.1 2.7 %collective-permute-start.2 = (bf16[128,1280]{1,0:T(8,128)(2,1)S(1)}, bf16[128,1280]{1,0:T(8,128)(2,1)S(1)}, u32[]{:S(2)}, u32[]{:S(2)}) collective-permute-start(bf16[128,1280]{1,0:T(8,128)(2,1)S(1)} %slice_bitcast_fusion), channel_id=1, source_target_pairs={{0,28},{2,30},{4,24},{6,26},{8,4},{10,6},{12,0},{14,2},{16,12},{18... | collective-permute-start | bytes 983048 | tf_op jit(solution)/shard_map/ppermute | solution.py:229
  6.9 1.0 %copy-done.7 = bf16[1,128,2048]{2,1,0:T(8,128)(2,1)S(1)} copy-done((bf16[1,128,2048]{2,1,0:T(8,128)(2,1)S(1)}, bf16[1,128,2048]{2,1,0:T(8,128)(2,1)}, u32[]{:S(2)}) %copy-start.7) | copy-done | bytes 524312
  7.9 0.7 copy-done.9
  8.6 0.7 copy-done.11
  9.3 0.3 shard_map.95.meta_ref.refs_0_
  9.6 0.8 %collective-permute-done.incoming_ref = bf16[128,2048]{1,0:T(8,128)(2,1)S(1)} collective-permute-done((bf16[128,2048]{1,0:T(8,128)(2,1)}, bf16[128,2048]{1,0:T(8,128)(2,1)S(1)}, u32[]{:S(2)}, u32[]{:S(2)}) %collective-permute-start) | collective-permute-done | bytes 524320 | tf_op jit(solution)/shard_map/ppermute | solution.py:238
  10.4 0.4 shard_map.96
  10.7 3.5 %collective-permute-start.4 = (bf16[72,2048]{1,0:T(8,128)(2,1)S(1)}, bf16[72,2048]{1,0:T(8,128)(2,1)S(1)}, u32[]{:S(2)}, u32[]{:S(2)}) collective-permute-start(bf16[72,2048]{1,0:T(8,128)(2,1)S(1)} %get-tuple-element.16), channel_id=1, source_target_pairs={{0,2},{2,0},{4,6},{6,4},{1,3},{3,1},{5,7},{7,5},{8,10},{10,8},{12,... | collective-permute-start | bytes 884744 | tf_op jit(solution)/shard_map/ppermute | solution.py:31
  14.2 1.1 %collective-permute-start.3 = (bf16[72,768]{1,0:T(8,128)(2,1)S(1)}, bf16[72,768]{1,0:T(8,128)(2,1)S(1)}, u32[]{:S(2)}, u32[]{:S(2)}) collective-permute-start(bf16[72,768]{1,0:T(8,128)(2,1)S(1)} %get-tuple-element.14), channel_id=1, source_target_pairs={{0,4},{2,6},{4,0},{6,2},{1,5},{3,7},{5,1},{7,3},{8,12},{10,14},{12... | collective-permute-start | bytes 331784 | tf_op jit(solution)/shard_map/ppermute | solution.py:31
  15.3 1.8 %collective-permute-start.1 = (f32[8,128]{1,0:T(8,128)S(1)}, f32[8,128]{1,0:T(8,128)S(1)}, u32[]{:S(2)}, u32[]{:S(2)}) collective-permute-start(f32[8,128]{1,0:T(8,128)S(1)} %shard_map.95.meta_ref.refs_0_), channel_id=1, source_target_pairs={{0,4},{2,6},{4,0},{6,2},{1,5},{3,7},{5,1},{7,3},{8,12},{10,14},{12... | collective-permute-start | bytes 12296 | tf_op jit(solution)/shard_map/ppermute | solution.py:31
  17.2 1.5 %copy-done = bf16[1,1,448,2048]{3,2,1,0:T(8,128)(2,1)S(1)} copy-done((bf16[1,1,448,2048]{3,2,1,0:T(8,128)(2,1)S(1)}, bf16[1,1,448,2048]{3,2,1,0:T(8,128)(2,1)}, u32[]{:S(2)}) %copy-start) | copy-done | bytes 1835032
  18.7 1.5 %copy-done.2 = bf16[1,1,448,2048]{3,2,1,0:T(8,128)(2,1)S(1)} copy-done((bf16[1,1,448,2048]{3,2,1,0:T(8,128)(2,1)S(1)}, bf16[1,1,448,2048]{3,2,1,0:T(8,128)(2,1)}, u32[]{:S(2)}) %copy-start.2) | copy-done | bytes 1835032
  20.2 1.5 %copy-done.4 = bf16[1,1,448,2048]{3,2,1,0:T(8,128)(2,1)S(1)} copy-done((bf16[1,1,448,2048]{3,2,1,0:T(8,128)(2,1)S(1)}, bf16[1,1,448,2048]{3,2,1,0:T(8,128)(2,1)}, u32[]{:S(2)}) %copy-start.4) | copy-done | bytes 1835032
  21.7 3.2 %collective-permute-done.1.meta_ref = f32[8,128]{1,0:T(8,128)S(1)} collective-permute-done((f32[8,128]{1,0:T(8,128)S(1)}, f32[8,128]{1,0:T(8,128)S(1)}, u32[]{:S(2)}, u32[]{:S(2)}) %collective-permute-start.1) | collective-permute-done | bytes 4128 | tf_op jit(solution)/shard_map/ppermute | solution.py:31
  24.9 0.0 collective-permute-done.2.raw_ref._raw
  24.9 0.2 shard_map.99
  25.1 2.9 %collective-permute-start.7 = (bf16[72,1280]{1,0:T(8,128)(2,1)S(1)}, bf16[72,1280]{1,0:T(8,128)(2,1)S(1)}, u32[]{:S(2)}, u32[]{:S(2)}) collective-permute-start(bf16[72,1280]{1,0:T(8,128)(2,1)S(1)} %shard_map.99), channel_id=1, source_target_pairs={{0,2},{2,0},{4,6},{6,4},{1,3},{3,1},{5,7},{7,5},{8,10},{10,8},{12,... | collective-permute-start | bytes 552968 | tf_op jit(solution)/shard_map/ppermute | solution.py:31
  28.1 0.2 shard_map.100
  28.2 0.0 copy-start.3
  28.3 0.0 copy-start.5
  28.3 3.0 %collective-permute-start.8 = (bf16[72,768]{1,0:T(8,128)(2,1)S(1)}, bf16[72,768]{1,0:T(8,128)(2,1)S(1)}, u32[]{:S(2)}, u32[]{:S(2)}) collective-permute-start(bf16[72,768]{1,0:T(8,128)(2,1)S(1)} %shard_map.100), channel_id=1, source_target_pairs={{0,6},{2,4},{4,2},{6,0},{1,7},{3,5},{5,3},{7,1},{8,14},{10,12},{12... | collective-permute-start | bytes 331784 | tf_op jit(solution)/shard_map/ppermute | solution.py:31
  31.2 0.0 collective-permute-done.3.tail_ref
  31.2 0.0 collective-permute-done.4.refs_1_
  31.2 2.0 %shard_map.97 = (bf16[72,2176]{1,0:T(8,128)(2,1)S(1)}, bf16[72,2176]{1,0:T(8,128)(2,1)S(1)}, bf16[72,2176]{1,0:T(8,128)(2,1)S(1)}) custom-call(s32[1]{0:T(128)} %bitcast.me_ref, bf16[4,72,896]{2,1,0:T(8,128)(2,1)S(1)} %bitcast.29, bf16[448,2048]{1,0:T(8,128)(2,1)S(1)} %bitcast.20, bf16[448,2048]{1,0:T(8,128)(2,1)S(1)} %bitcast.23, ...), custom_call_target="tpu_custom_call" | custom-call | flops 1189085184 | bytes 7274496 | tf_op jit(solution)/shard_map/pallas_call | solution.py:279
  33.2 1.2 %collective-permute-start.5 = (bf16[72,2176]{1,0:T(8,128)(2,1)S(1)}, bf16[72,2176]{1,0:T(8,128)(2,1)S(1)}, u32[]{:S(2)}, u32[]{:S(2)}) collective-permute-start(bf16[72,2176]{1,0:T(8,128)(2,1)S(1)} %get-tuple-element.18), channel_id=1, source_target_pairs={{0,2},{2,0},{4,6},{6,4},{1,3},{3,1},{5,7},{7,5},{8,10},{10,8},{12,... | collective-permute-start | bytes 940040 | tf_op jit(solution)/shard_map/ppermute | solution.py:31
  34.4 1.7 %collective-permute-start.6 = (bf16[72,2176]{1,0:T(8,128)(2,1)S(1)}, bf16[72,2176]{1,0:T(8,128)(2,1)S(1)}, u32[]{:S(2)}, u32[]{:S(2)}) collective-permute-start(bf16[72,2176]{1,0:T(8,128)(2,1)S(1)} %get-tuple-element.19), channel_id=1, source_target_pairs={{0,4},{2,6},{4,0},{6,2},{1,5},{3,7},{5,1},{7,3},{8,12},{10,14},{12... | collective-permute-start | bytes 940040 | tf_op jit(solution)/shard_map/ppermute | solution.py:31
  36.1 2.7 %collective-permute-done.8.refs_1_ = bf16[72,768]{1,0:T(8,128)(2,1)S(1)} collective-permute-done((bf16[72,768]{1,0:T(8,128)(2,1)S(1)}, bf16[72,768]{1,0:T(8,128)(2,1)S(1)}, u32[]{:S(2)}, u32[]{:S(2)}) %collective-permute-start.8) | collective-permute-done | bytes 110624 | tf_op jit(solution)/shard_map/ppermute | solution.py:31
  38.8 0.0 collective-permute-done.7.refs_0_
  38.8 0.0 copy-start.8
  38.8 0.0 copy-start.10
  38.9 1.6 %shard_map.101 = (bf16[72,1536]{1,0:T(8,128)(2,1)S(1)}, bf16[72,640]{1,0:T(8,128)(2,1)S(1)}) custom-call(s32[1]{0:T(128)} %bitcast.me_ref, bf16[4,72,896]{2,1,0:T(8,128)(2,1)S(1)} %bitcast.30, bf16[448,2048]{1,0:T(8,128)(2,1)S(1)} %bitcast.21, bf16[448,2048]{1,0:T(8,128)(2,1)S(1)} %bitcast.24, bf16[448,2048]{1,0:T(8,128)(2,1)S(1)} %bitcast.27, ...), custom_call_target="tpu_custom_call" | custom-call | flops 396361728 | bytes 6094848 | tf_op jit(solution)/shard_map/pallas_call | solution.py:288
  40.4 8.1 %collective-permute-start.9 = (bf16[72,1536]{1,0:T(8,128)(2,1)S(1)}, bf16[72,1536]{1,0:T(8,128)(2,1)S(1)}, u32[]{:S(2)}, u32[]{:S(2)}) collective-permute-start(bf16[72,1536]{1,0:T(8,128)(2,1)S(1)} %get-tuple-element.20), channel_id=1, source_target_pairs={{0,6},{2,4},{4,2},{6,0},{1,7},{3,5},{5,3},{7,1},{8,14},{10,12},{12... | collective-permute-start | bytes 663560 | tf_op jit(solution)/shard_map/ppermute | solution.py:31
  48.5 7.9 %collective-permute-done.9.refs_3_ = bf16[72,1536]{1,0:T(8,128)(2,1)S(1)} collective-permute-done((bf16[72,1536]{1,0:T(8,128)(2,1)S(1)}, bf16[72,1536]{1,0:T(8,128)(2,1)S(1)}, u32[]{:S(2)}, u32[]{:S(2)}) %collective-permute-start.9) | collective-permute-done | bytes 221216 | tf_op jit(solution)/shard_map/ppermute | solution.py:31
  56.4 0.0 collective-permute-done.5.refs_1_
  56.4 0.7 collective-permute-done.6.refs_2_
  57.1 0.9 %shard_map.102 = (f32[4,2048]{1,0:T(4,128)S(1)}, f32[128,2048]{1,0:T(8,128)S(1)}) custom-call(f32[8,128]{1,0:T(8,128)S(1)} %shard_map.95.meta_ref.refs_0_, bf16[128,2048]{1,0:T(8,128)(2,1)S(1)} %bitcast.32, bf16[128,2048]{1,0:T(8,128)(2,1)S(1)} %collective-permute-done.incoming_ref, bf16[4,2048]{1,0:T(4,128)(2,1)S(1)} %bitcast.34, ...), custom_call_target="tpu_custom_call" | custom-call | flops 150994944 | bytes 3276800 | tf_op jit(solution)/shard_map/pallas_call | solution.py:298
  58.1 1.6 %collective-permute-start.11 = (f32[4,2048]{1,0:T(4,128)S(1)}, f32[4,2048]{1,0:T(4,128)S(1)}, u32[]{:S(2)}, u32[]{:S(2)}) collective-permute-start(f32[4,2048]{1,0:T(4,128)S(1)} %get-tuple-element.23), channel_id=1, source_target_pairs={{0,1},{1,0},{2,3},{3,2},{4,5},{5,4},{6,7},{7,6},{8,9},{9,8},{10,11... | collective-permute-start | bytes 98312 | tf_op jit(solution)/shard_map/ppermute | solution.py:31
  59.6 1.4 %collective-permute-start.10 = (bf16[72,640]{1,0:T(8,128)(2,1)S(1)}, bf16[72,640]{1,0:T(8,128)(2,1)S(1)}, u32[]{:S(2)}, u32[]{:S(2)}) collective-permute-start(bf16[72,640]{1,0:T(8,128)(2,1)S(1)} %get-tuple-element.22), channel_id=1, source_target_pairs={{0,6},{2,4},{4,2},{6,0},{1,7},{3,5},{5,3},{7,1},{8,14},{10,12},{12... | collective-permute-start | bytes 276488 | tf_op jit(solution)/shard_map/ppermute | solution.py:31
  61.0 1.1 %collective-permute-done.11 = f32[4,2048]{1,0:T(4,128)S(1)} collective-permute-done((f32[4,2048]{1,0:T(4,128)S(1)}, f32[4,2048]{1,0:T(4,128)S(1)}, u32[]{:S(2)}, u32[]{:S(2)}) %collective-permute-start.11) | collective-permute-done | bytes 32800 | tf_op jit(solution)/shard_map/ppermute | solution.py:31
  62.1 1.5 %collective-permute-start.14 = (bf16[4,2048]{1,0:T(4,128)(2,1)S(1)}, bf16[4,2048]{1,0:T(4,128)(2,1)S(1)}, u32[]{:S(2)}, u32[]{:S(2)}) collective-permute-start(bf16[4,2048]{1,0:T(4,128)(2,1)S(1)} %get-tuple-element.26), channel_id=1, source_target_pairs={{0,6},{2,4},{4,2},{6,0},{1,7},{3,5},{5,3},{7,1},{8,14},{10,12},{12... | collective-permute-start | bytes 49160 | tf_op jit(solution)/shard_map/ppermute | solution.py:31
  63.5 4.6 %collective-permute-start.13 = (bf16[4,2048]{1,0:T(4,128)(2,1)S(1)}, bf16[4,2048]{1,0:T(4,128)(2,1)S(1)}, u32[]{:S(2)}, u32[]{:S(2)}) collective-permute-start(bf16[4,2048]{1,0:T(4,128)(2,1)S(1)} %get-tuple-element.26), channel_id=1, source_target_pairs={{0,4},{2,6},{4,0},{6,2},{1,5},{3,7},{5,1},{7,3},{8,12},{10,14},{12... | collective-permute-start | bytes 49160 | tf_op jit(solution)/shard_map/ppermute | solution.py:31
  68.1 0.0 collective-permute-done.10.refs_0_
  68.1 0.0 collective-permute-done.14.refs_4_
  68.1 1.9 %collective-permute-done.13.refs_3_ = bf16[4,2048]{1,0:T(4,128)(2,1)S(1)} collective-permute-done((bf16[4,2048]{1,0:T(4,128)(2,1)S(1)}, bf16[4,2048]{1,0:T(4,128)(2,1)S(1)}, u32[]{:S(2)}, u32[]{:S(2)}) %collective-permute-start.13) | collective-permute-done | bytes 16416 | tf_op jit(solution)/shard_map/ppermute | solution.py:31
  70.0 1.9 %collective-permute-done.12.refs_2_ = bf16[4,2048]{1,0:T(4,128)(2,1)S(1)} collective-permute-done((bf16[4,2048]{1,0:T(4,128)(2,1)S(1)}, bf16[4,2048]{1,0:T(4,128)(2,1)S(1)}, u32[]{:S(2)}, u32[]{:S(2)}) %collective-permute-start.12) | collective-permute-done | bytes 16416 | tf_op jit(solution)/shard_map/ppermute | solution.py:31
  71.9 1.0 %shard_map.103 = (bf16[128,2048]{1,0:T(8,128)(2,1)}, f32[4,2048]{1,0:T(4,128)}) custom-call(f32[8,128]{1,0:T(8,128)S(1)} %shard_map.95.meta_ref.refs_0_, f32[128,2048]{1,0:T(8,128)S(1)} %get-tuple-element.21.base_ref, bf16[72,640]{1,0:T(8,128)(2,1)S(1)} %collective-permute-done.10.refs_0_, f32[4,2048]{1,0:T(4,128)S(1)} %get-tuple-element.27.refs_1_, ...), custom_call_target="tpu_custom_call" | custom-call | flops 37748736 | bytes 1867776 | tf_op jit(solution)/shard_map/pallas_call | solution.py:316
  (17 shorter events, 0.0 us)
Async XLA Ops:
  0.6 16.5 %copy-start.6 = (bf16[1,1,288,896]{3,2,1,0:T(8,128)(2,1)S(1)}, bf16[1,1,288,896]{3,2,1,0:T(8,128)(2,1)}, u32[]{:S(2)}) copy-start(bf16[1,1,288,896]{3,2,1,0:T(8,128)(2,1)} %param.15) | copy-start | bytes 1548292
  0.6 9.7 %collective-permute-start = (bf16[128,2048]{1,0:T(8,128)(2,1)}, bf16[128,2048]{1,0:T(8,128)(2,1)S(1)}, u32[]{:S(2)}, u32[]{:S(2)}) collective-permute-start(bf16[128,2048]{1,0:T(8,128)(2,1)} %bitcast.36), channel_id=1, source_target_pairs={{0,24},{8,0},{16,8},{24,16},{1,25},{9,1},{17,9},{25,17},{2,26},{10... | collective-permute-start | bytes 1572872 | tf_op jit(solution)/shard_map/ppermute | solution.py:238
  4.1 20.8 %collective-permute-start.2 = (bf16[128,1280]{1,0:T(8,128)(2,1)S(1)}, bf16[128,1280]{1,0:T(8,128)(2,1)S(1)}, u32[]{:S(2)}, u32[]{:S(2)}) collective-permute-start(bf16[128,1280]{1,0:T(8,128)(2,1)S(1)} %slice_bitcast_fusion), channel_id=1, source_target_pairs={{0,28},{2,30},{4,24},{6,26},{8,4},{10,6},{12,0},{14,2},{16,12},{18... | collective-permute-start | bytes 983048 | tf_op jit(solution)/shard_map/ppermute | solution.py:229
  6.8 1.0 %copy-start.7 = (bf16[1,128,2048]{2,1,0:T(8,128)(2,1)S(1)}, bf16[1,128,2048]{2,1,0:T(8,128)(2,1)}, u32[]{:S(2)}) copy-start(bf16[1,128,2048]{2,1,0:T(8,128)(2,1)} %param.9) | copy-start | bytes 1572868
  7.9 0.7 copy-start.9
  8.6 0.7 copy-start.11
  10.7 20.5 %collective-permute-start.4 = (bf16[72,2048]{1,0:T(8,128)(2,1)S(1)}, bf16[72,2048]{1,0:T(8,128)(2,1)S(1)}, u32[]{:S(2)}, u32[]{:S(2)}) collective-permute-start(bf16[72,2048]{1,0:T(8,128)(2,1)S(1)} %get-tuple-element.16), channel_id=1, source_target_pairs={{0,2},{2,0},{4,6},{6,4},{1,3},{3,1},{5,7},{7,5},{8,10},{10,8},{12,... | collective-permute-start | bytes 884744 | tf_op jit(solution)/shard_map/ppermute | solution.py:31
  14.2 17.0 %collective-permute-start.3 = (bf16[72,768]{1,0:T(8,128)(2,1)S(1)}, bf16[72,768]{1,0:T(8,128)(2,1)S(1)}, u32[]{:S(2)}, u32[]{:S(2)}) collective-permute-start(bf16[72,768]{1,0:T(8,128)(2,1)S(1)} %get-tuple-element.14), channel_id=1, source_target_pairs={{0,4},{2,6},{4,0},{6,2},{1,5},{3,7},{5,1},{7,3},{8,12},{10,14},{12... | collective-permute-start | bytes 331784 | tf_op jit(solution)/shard_map/ppermute | solution.py:31
  15.3 9.6 %collective-permute-start.1 = (f32[8,128]{1,0:T(8,128)S(1)}, f32[8,128]{1,0:T(8,128)S(1)}, u32[]{:S(2)}, u32[]{:S(2)}) collective-permute-start(f32[8,128]{1,0:T(8,128)S(1)} %shard_map.95.meta_ref.refs_0_), channel_id=1, source_target_pairs={{0,4},{2,6},{4,0},{6,2},{1,5},{3,7},{5,1},{7,3},{8,12},{10,14},{12... | collective-permute-start | bytes 12296 | tf_op jit(solution)/shard_map/ppermute | solution.py:31
  17.2 1.5 %copy-start = (bf16[1,1,448,2048]{3,2,1,0:T(8,128)(2,1)S(1)}, bf16[1,1,448,2048]{3,2,1,0:T(8,128)(2,1)}, u32[]{:S(2)}) copy-start(bf16[1,1,448,2048]{3,2,1,0:T(8,128)(2,1)} %param.12) | copy-start | bytes 5505028
  18.7 1.5 %copy-start.2 = (bf16[1,1,448,2048]{3,2,1,0:T(8,128)(2,1)S(1)}, bf16[1,1,448,2048]{3,2,1,0:T(8,128)(2,1)}, u32[]{:S(2)}) copy-start(bf16[1,1,448,2048]{3,2,1,0:T(8,128)(2,1)} %param.13) | copy-start | bytes 5505028
  20.2 1.5 %copy-start.4 = (bf16[1,1,448,2048]{3,2,1,0:T(8,128)(2,1)S(1)}, bf16[1,1,448,2048]{3,2,1,0:T(8,128)(2,1)}, u32[]{:S(2)}) copy-start(bf16[1,1,448,2048]{3,2,1,0:T(8,128)(2,1)} %param.14) | copy-start | bytes 5505028
  21.7 9.6 %copy-start.1 = (bf16[1,1,448,2048]{3,2,1,0:T(8,128)(2,1)S(1)}, bf16[1,1,448,2048]{3,2,1,0:T(8,128)(2,1)}, u32[]{:S(2)}) copy-start(bf16[1,1,448,2048]{3,2,1,0:T(8,128)(2,1)} %param.12) | copy-start | bytes 5505028
  25.1 13.7 %collective-permute-start.7 = (bf16[72,1280]{1,0:T(8,128)(2,1)S(1)}, bf16[72,1280]{1,0:T(8,128)(2,1)S(1)}, u32[]{:S(2)}, u32[]{:S(2)}) collective-permute-start(bf16[72,1280]{1,0:T(8,128)(2,1)S(1)} %shard_map.99), channel_id=1, source_target_pairs={{0,2},{2,0},{4,6},{6,4},{1,3},{3,1},{5,7},{7,5},{8,10},{10,8},{12,... | collective-permute-start | bytes 552968 | tf_op jit(solution)/shard_map/ppermute | solution.py:31
  28.2 10.6 %copy-start.3 = (bf16[1,1,448,2048]{3,2,1,0:T(8,128)(2,1)S(1)}, bf16[1,1,448,2048]{3,2,1,0:T(8,128)(2,1)}, u32[]{:S(2)}) copy-start(bf16[1,1,448,2048]{3,2,1,0:T(8,128)(2,1)} %param.13) | copy-start | bytes 5505028
  28.3 10.6 %copy-start.5 = (bf16[1,1,448,2048]{3,2,1,0:T(8,128)(2,1)S(1)}, bf16[1,1,448,2048]{3,2,1,0:T(8,128)(2,1)}, u32[]{:S(2)}) copy-start(bf16[1,1,448,2048]{3,2,1,0:T(8,128)(2,1)} %param.14) | copy-start | bytes 5505028
  28.3 10.5 %collective-permute-start.8 = (bf16[72,768]{1,0:T(8,128)(2,1)S(1)}, bf16[72,768]{1,0:T(8,128)(2,1)S(1)}, u32[]{:S(2)}, u32[]{:S(2)}) collective-permute-start(bf16[72,768]{1,0:T(8,128)(2,1)S(1)} %shard_map.100), channel_id=1, source_target_pairs={{0,6},{2,4},{4,2},{6,0},{1,7},{3,5},{5,3},{7,1},{8,14},{10,12},{12... | collective-permute-start | bytes 331784 | tf_op jit(solution)/shard_map/ppermute | solution.py:31
  33.2 23.2 %collective-permute-start.5 = (bf16[72,2176]{1,0:T(8,128)(2,1)S(1)}, bf16[72,2176]{1,0:T(8,128)(2,1)S(1)}, u32[]{:S(2)}, u32[]{:S(2)}) collective-permute-start(bf16[72,2176]{1,0:T(8,128)(2,1)S(1)} %get-tuple-element.18), channel_id=1, source_target_pairs={{0,2},{2,0},{4,6},{6,4},{1,3},{3,1},{5,7},{7,5},{8,10},{10,8},{12,... | collective-permute-start | bytes 940040 | tf_op jit(solution)/shard_map/ppermute | solution.py:31
  34.4 22.7 %collective-permute-start.6 = (bf16[72,2176]{1,0:T(8,128)(2,1)S(1)}, bf16[72,2176]{1,0:T(8,128)(2,1)S(1)}, u32[]{:S(2)}, u32[]{:S(2)}) collective-permute-start(bf16[72,2176]{1,0:T(8,128)(2,1)S(1)} %get-tuple-element.19), channel_id=1, source_target_pairs={{0,4},{2,6},{4,0},{6,2},{1,5},{3,7},{5,1},{7,3},{8,12},{10,14},{12... | collective-permute-start | bytes 940040 | tf_op jit(solution)/shard_map/ppermute | solution.py:31
  38.8 18.3 %copy-start.8 = (bf16[1,128,2048]{2,1,0:T(8,128)(2,1)S(1)}, bf16[1,128,2048]{2,1,0:T(8,128)(2,1)}, u32[]{:S(2)}) copy-start(bf16[1,128,2048]{2,1,0:T(8,128)(2,1)} %param.9) | copy-start | bytes 1572868
  38.8 18.3 %copy-start.10 = (bf16[1,2048,4]{1,2,0:T(4,128)(2,1)S(1)}, bf16[1,2048,4]{1,2,0:T(4,128)(2,1)}, u32[]{:S(2)}) copy-start(bf16[1,2048,4]{1,2,0:T(4,128)(2,1)} %param.11) | copy-start | bytes 49156
  40.4 16.0 %collective-permute-start.9 = (bf16[72,1536]{1,0:T(8,128)(2,1)S(1)}, bf16[72,1536]{1,0:T(8,128)(2,1)S(1)}, u32[]{:S(2)}, u32[]{:S(2)}) collective-permute-start(bf16[72,1536]{1,0:T(8,128)(2,1)S(1)} %get-tuple-element.20), channel_id=1, source_target_pairs={{0,6},{2,4},{4,2},{6,0},{1,7},{3,5},{5,3},{7,1},{8,14},{10,12},{12... | collective-permute-start | bytes 663560 | tf_op jit(solution)/shard_map/ppermute | solution.py:31
  58.1 4.0 %collective-permute-start.11 = (f32[4,2048]{1,0:T(4,128)S(1)}, f32[4,2048]{1,0:T(4,128)S(1)}, u32[]{:S(2)}, u32[]{:S(2)}) collective-permute-start(f32[4,2048]{1,0:T(4,128)S(1)} %get-tuple-element.23), channel_id=1, source_target_pairs={{0,1},{1,0},{2,3},{3,2},{4,5},{5,4},{6,7},{7,6},{8,9},{9,8},{10,11... | collective-permute-start | bytes 98312 | tf_op jit(solution)/shard_map/ppermute | solution.py:31
  59.6 8.5 %collective-permute-start.10 = (bf16[72,640]{1,0:T(8,128)(2,1)S(1)}, bf16[72,640]{1,0:T(8,128)(2,1)S(1)}, u32[]{:S(2)}, u32[]{:S(2)}) collective-permute-start(bf16[72,640]{1,0:T(8,128)(2,1)S(1)} %get-tuple-element.22), channel_id=1, source_target_pairs={{0,6},{2,4},{4,2},{6,0},{1,7},{3,5},{5,3},{7,1},{8,14},{10,12},{12... | collective-permute-start | bytes 276488 | tf_op jit(solution)/shard_map/ppermute | solution.py:31
  62.1 6.1 %collective-permute-start.14 = (bf16[4,2048]{1,0:T(4,128)(2,1)S(1)}, bf16[4,2048]{1,0:T(4,128)(2,1)S(1)}, u32[]{:S(2)}, u32[]{:S(2)}) collective-permute-start(bf16[4,2048]{1,0:T(4,128)(2,1)S(1)} %get-tuple-element.26), channel_id=1, source_target_pairs={{0,6},{2,4},{4,2},{6,0},{1,7},{3,5},{5,3},{7,1},{8,14},{10,12},{12... | collective-permute-start | bytes 49160 | tf_op jit(solution)/shard_map/ppermute | solution.py:31
  63.5 6.5 %collective-permute-start.13 = (bf16[4,2048]{1,0:T(4,128)(2,1)S(1)}, bf16[4,2048]{1,0:T(4,128)(2,1)S(1)}, u32[]{:S(2)}, u32[]{:S(2)}) collective-permute-start(bf16[4,2048]{1,0:T(4,128)(2,1)S(1)} %get-tuple-element.26), channel_id=1, source_target_pairs={{0,4},{2,6},{4,0},{6,2},{1,5},{3,7},{5,1},{7,3},{8,12},{10,14},{12... | collective-permute-start | bytes 49160 | tf_op jit(solution)/shard_map/ppermute | solution.py:31
  68.1 3.7 %collective-permute-start.12 = (bf16[4,2048]{1,0:T(4,128)(2,1)S(1)}, bf16[4,2048]{1,0:T(4,128)(2,1)S(1)}, u32[]{:S(2)}, u32[]{:S(2)}) collective-permute-start(bf16[4,2048]{1,0:T(4,128)(2,1)S(1)} %get-tuple-element.26), channel_id=1, source_target_pairs={{0,2},{2,0},{4,6},{6,4},{1,3},{3,1},{5,7},{7,5},{8,10},{10,8},{12,... | collective-permute-start | bytes 49160 | tf_op jit(solution)/shard_map/ppermute | solution.py:31

commit v3 on v2

--- a/solution.py
+++ b/solution.py
@@ -13,6 +13,7 @@
 ANY = pl.BlockSpec(memory_space=pl.ANY)
 SMEM = pl.BlockSpec(memory_space=pltpu.SMEM)
 LANES = 128
+MARK = 16
 
 
 def call(kernel, out_shape, specs, flops, size):
@@ -109,66 +110,68 @@
     return grad, jnp.broadcast_to(scores.astype(F32), (rows.shape[0], LANES))
 
 
+def mark_of(width):
+    return width % LANES or LANES
+
+
+def written(aways, grad, spread, out_refs):
+    out_refs = list(out_refs)
+    features = grad.shape[1]
+    for at in range(len(aways)):
+        done = 0
+        while done < features:
+            ref = out_refs.pop(0)
+            capacity, width = ref.shape
+            part = slice(at * capacity, (at + 1) * capacity)
+            if done == 0:
+                mark = mark_of(width)
+                width = width - mark
+                ref[:, width:] = spread[part, :mark].astype(BF16)
+            ref[:, :width] = grad[part, done : done + width].astype(BF16)
+            done = done + width
+
+
 def first_kernel(
-    aways, me_ref, pre_ref, gate_ref, up_ref, down_ref, meta_ref, raw_ref, tail_ref, *refs
+    aways, me_ref, pre_ref, gate_ref, up_ref, down_ref, meta_ref, raw_ref, tail_ref, own_ref, *out_refs
 ):
-    count = len(aways)
-    row_refs, out_refs = refs[: count - 1], refs[count - 1 :]
+    me = me_ref[0]
     capacity = tail_ref.shape[0]
-    me = me_ref[0]
     head = packed_rows(meta_ref[...], raw_ref[...], aways[-1], capacity).astype(F32)
     far = jnp.concatenate([head, tail_ref[...].astype(F32)], axis=1)
-    rows = jnp.concatenate([ref[...].astype(F32) for ref in row_refs] + [far], axis=0).astype(BF16)
+    rows = jnp.concatenate([own_ref[...].astype(F32), far], axis=0).astype(BF16)
     pre = jnp.concatenate([pre_ref[me ^ away].astype(F32) for away in aways], axis=0)
     grad, spread = swiglu_grads(rows, pre, gate_ref, up_ref, down_ref)
-    features = grad.shape[1]
-    for at in range(count):
-        part = slice(at * capacity, (at + 1) * capacity)
-        out_refs[at][:, :features] = grad[part].astype(BF16)
-        out_refs[at][:, features:] = spread[part].astype(BF16)
-
-
-def last_kernel(aways, early, me_ref, pre_ref, gate_ref, up_ref, down_ref, _, *refs):
-    count = len(aways)
-    head_refs, tail_refs, out_refs = refs[:count], refs[count : 2 * count], refs[2 * count :]
-    capacity = head_refs[0].shape[0]
+    written(aways, grad, spread, out_refs)
+
+
+def last_kernel(aways, near, me_ref, pre_ref, gate_ref, up_ref, down_ref, _, *refs):
     me = me_ref[0]
-    rows = [
-        jnp.concatenate([head[...].astype(F32), tail[...].astype(F32)], axis=1)
-        for head, tail in zip(head_refs, tail_refs)
-    ]
+    rows = [ref[...].astype(F32) for ref in refs[:near]]
+    far = len(aways) - near
+    for head, tail in zip(refs[near : near + far], refs[near + far : near + 2 * far]):
+        rows.append(jnp.concatenate([head[...].astype(F32), tail[...].astype(F32)], axis=1))
     rows = jnp.concatenate(rows, axis=0).astype(BF16)
     pre = jnp.concatenate([pre_ref[me ^ away].astype(F32) for away in aways], axis=0)
     grad, spread = swiglu_grads(rows, pre, gate_ref, up_ref, down_ref)
-    for at in range(count):
-        part = slice(at * capacity, (at + 1) * capacity)
-        out_refs[at][:, :early] = grad[part, :early].astype(BF16)
-        out_refs[at][:, early:] = spread[part].astype(BF16)
-        out_refs[count + at][...] = grad[part, early:].astype(BF16)
-
-
-def mixed_rows(meta, aways, refs, width):
-    total = 0.0
-    for away, ref in zip(aways, refs):
-        first, second = slots_of(meta, away, ref.shape[0])
-        pick = jnp.where(first | second, 1.0, 0.0).astype(BF16)
-        total = total + lax.dot_general(
-            pick, ref[:, :width], (((0,), (0,)), ((), ())), preferred_element_type=F32
-        )
-    return total
-
-
-def logit_kernel(whole, last, meta_ref, inputs_ref, incoming_ref, router_ref, *refs):
-    whole_refs, last_refs = refs[: len(whole)], refs[len(whole) : -2]
-    partial_ref, base_ref = refs[-2], refs[-1]
+    written(aways, grad, spread, refs[near + 2 * far :])
+
+
+def mixed_rows(meta, away, values):
+    first, second = slots_of(meta, away, values.shape[0])
+    pick = jnp.where(first | second, 1.0, 0.0).astype(BF16)
+    return lax.dot_general(pick, values, (((0,), (0,)), ((), ())), preferred_element_type=F32)
+
+
+def logit_kernel(meta_ref, inputs_ref, incoming_ref, router_ref, *refs):
+    head_refs, partial_ref, base_ref = refs[:-2], refs[-2], refs[-1]
     meta = meta_ref[...]
-    tokens, features = incoming_ref.shape
+    tokens = meta.shape[1]
     pair_0 = jnp.zeros((1, tokens), F32)
     pair_1 = jnp.zeros((1, tokens), F32)
-    for away, ref in zip(list(whole) + list(last), refs[:-2]):
+    for away, ref in enumerate(head_refs):
         capacity, width = ref.shape
         first, second = slots_of(meta, away, capacity)
-        score = ref[:, width - LANES :].astype(F32)[:, 0:1]
+        score = ref[:, width - mark_of(width) :].astype(F32)[:, 0:1]
         pair_0 = pair_0 + jnp.sum(jnp.where(first, score, 0.0), axis=0, keepdims=True)
         pair_1 = pair_1 + jnp.sum(jnp.where(second, score, 0.0), axis=0, keepdims=True)
     total = pair_0 + pair_1
@@ -181,20 +184,22 @@
     through = lax.dot_general(
         grad, router_ref[...], (((0,), (0,)), ((), ())), preferred_element_type=F32
     )
-    base = incoming_ref[...].astype(F32) + through + mixed_rows(meta, whole, whole_refs, features)
-    split = last_refs[0].shape[1] - LANES
-    base_ref[:, :split] = base[:, :split] + mixed_rows(meta, last, last_refs, split)
-    base_ref[:, split:] = base[:, split:]
+    base_ref[...] = incoming_ref[...].astype(F32) + through
+    for away, ref in enumerate(head_refs):
+        width = ref.shape[1] - mark_of(ref.shape[1])
+        base_ref[:, :width] += mixed_rows(meta, away, ref[:, :width])
 
 
 def final_kernel(aways, count, meta_ref, base_ref, *refs):
-    out_ref, router_ref = refs[-2], refs[-1]
-    width = refs[0].shape[1]
-    split = out_ref.shape[1] - width
-    out_ref[:, :split] = base_ref[:, :split].astype(out_ref.dtype)
-    total = base_ref[:, split:] + mixed_rows(meta_ref[...], aways, refs[: len(aways)], width)
-    out_ref[:, split:] = total.astype(out_ref.dtype)
-    parts = [ref[...].astype(F32) for ref in refs[len(aways) : -2]]
+    part_refs, (out_ref, router_ref) = refs[len(aways) : -2], refs[-2:]
+    meta = meta_ref[...]
+    done = out_ref.shape[1] - refs[0].shape[1]
+    total = base_ref[:, done:]
+    for away, ref in zip(aways, refs):
+        total = total + mixed_rows(meta, away, ref[...])
+    out_ref[:, :done] = base_ref[:, :done].astype(out_ref.dtype)
+    out_ref[:, done:] = total.astype(out_ref.dtype)
+    parts = [ref[...].astype(F32) for ref in part_refs]
     router_ref[...] = sum(parts[1:], parts[0]) / float(count)
 
 
@@ -214,7 +219,7 @@
     pre = saved_preacts[0, 0].reshape(sources, capacity, 2 * hidden)
     half = sources // 2
     split = features * 5 // 8
-    early = features * 11 // 16
+    early = features * 7 // 16
     near, last = list(range(half)), list(range(half + 1, sources))
 
     def shape(rows, columns, kind=BF16):
@@ -272,36 +277,49 @@
         pick_flops * len(last),
         tokens * features * 2 + block_bytes * len(last),
     )(held, far_meta, raw)
-    tails = [exchanged(value, "expert", away) for away, value in zip(last, late)]
-    heads = [exchanged(value, "expert", away - half) for away, value in zip(last, relays)]
-
-    whole = near + [half]
+    tails_of_last = [exchanged(value, "expert", away) for away, value in zip(last, late)]
+    relayed_heads = [exchanged(value, "expert", away - half) for away, value in zip(last, relays)]
+
+    others = near[1:] + last
+
+    def widths_of(away):
+        if away > half:
+            return [early + LANES, features - early]
+        return [features + (MARK if 0 < away < half else LANES)]
+
+    heads, tails = {}, {}
+
+    def returned(aways, values):
+        values = list(values)
+        for away in aways:
+            for width, into in zip(widths_of(away), (heads, tails)):
+                value = values.pop(0)
+                into[away] = exchanged(value, "expert", away) if away else value
+
     first = call(
-        functools.partial(first_kernel, whole),
-        [shape(capacity, features + LANES)] * len(whole),
-        [SMEM] + [VMEM] * (7 + half),
-        row_flops * len(whole),
-        weight_bytes + 2 * block_bytes * len(whole),
-    )(me, pre, gate, up, down, far_meta, raw, far_tail, *rows)
-    back = [exchanged(value, "expert", away) if away else value for away, value in zip(whole, first)]
-
+        functools.partial(first_kernel, [0, half]),
+        [shape(capacity, width) for away in (0, half) for width in widths_of(away)],
+        [SMEM] + [VMEM] * 8,
+        row_flops * 2,
+        weight_bytes + 4 * block_bytes,
+    )(me, pre, gate, up, down, far_meta, raw, far_tail, rows[0])
+    returned([0, half], first)
     ends = call(
-        functools.partial(last_kernel, last, early),
-        [shape(capacity, early + LANES)] * len(last) + [shape(capacity, features - early)] * len(last),
-        [SMEM] + [VMEM] * 4 + [ANY] + [VMEM] * (2 * len(last)),
-        row_flops * len(last),
-        weight_bytes + 2 * block_bytes * len(last),
-    )(me, pre, gate, up, down, first[0], *heads, *tails)
-    back_heads = [exchanged(value, "expert", away) for away, value in zip(last, ends)]
-    back_tails = [exchanged(value, "expert", away) for away, value in zip(last, ends[len(last) :])]
+        functools.partial(last_kernel, others, half - 1),
+        [shape(capacity, width) for away in others for width in widths_of(away)],
+        [SMEM] + [VMEM] * 4 + [ANY] + [VMEM] * (half - 1 + 2 * len(last)),
+        row_flops * len(others),
+        weight_bytes + 2 * block_bytes * len(others),
+    )(me, pre, gate, up, down, first[0], *rows[1:], *relayed_heads, *tails_of_last)
+    returned(others, ends)
 
     partial, base = call(
-        functools.partial(logit_kernel, whole, last),
+        logit_kernel,
         [shape(experts, features, F32), shape(tokens, features, F32)],
         [VMEM] * (4 + sources),
         pick_flops * sources,
         tokens * features * 8 + block_bytes * sources,
-    )(meta, inputs, incoming, router, *back, *back_heads)
+    )(meta, inputs, incoming, router, *[heads[away] for away in range(sources)])
     step = 1
     while step < replicas:
         partial = partial + exchanged(partial, "dp", step)
@@ -312,14 +330,13 @@
         step *= 2
     sent = partial.astype(BF16)
     parts = [partial] + [exchanged(sent, "expert", away) for away in range(step, sources, step)]
-
     result, router_grad = call(
-        functools.partial(final_kernel, last, tokens * sources * replicas),
+        functools.partial(final_kernel, sorted(tails), tokens * sources * replicas),
         [shape(tokens, features), shape(experts, features, F32)],
-        [VMEM] * (2 + len(last) + len(parts)),
-        pick_flops * len(last),
-        tokens * features * 6 + block_bytes * len(last),
-    )(meta, base, *back_tails, *parts)
+        [VMEM] * (2 + len(tails) + len(parts)),
+        pick_flops * len(tails),
+        tokens * features * 6 + block_bytes * len(tails),
+    )(meta, base, *[tails[away] for away in sorted(tails)], *parts)
     return (result[None], router_grad.T[None])
 
 

time: 73.3 us -> 71.3 us (0.973)
  starting transfers between devices: 37.5 us -> 27.8 us
  waiting for transfers between devices: 20.2 us -> 27.9 us
    ppermute x13, starting transfers between devices: 32.3 us -> 22.6 us  [exchanged(): lax.ppermute(value, axis, [(at, at ^ distance) for at in range(count)])]
    ppermute x13, waiting for transfers between devices: 19.3 us -> 27.1 us  [exchanged(): lax.ppermute(value, axis, [(at, at ^ distance) for at in range(count)])]
  transfers between devices with their start and end apart: 15 -> 15, of which waited for: 8 -> 10; matrix products, arithmetic and copies ran while one was open for 1% -> 1% of each run, Pallas kernels for 6% -> 6%
where the time goes in v3:
time: 71.3 us; the launch traced here: 70.9 us
  waiting for transfers between devices  27.9 us (39%)
  starting transfers between devices  27.8 us (39%)
  local copies, waits for them, and re-layouts  7.99 us (11%)
  Pallas kernels  6.45 us (9%)
  between operations  0.76 us (1%)
    ppermute x13, waiting for transfers between devices, exchanged(): lax.ppermute(value, axis, [(at, at ^ distance) for at in range(count)])  27.1 us
    ppermute x13, starting transfers between devices, exchanged(): lax.ppermute(value, axis, [(at, at ^ distance) for at in range(count)])  22.6 us
    unnamed x24, local copies, waits for them, and re-layouts  6.97 us
    ppermute x1, starting transfers between devices, shards(): lax.ppermute(upstream[0, :, :split], ('pipe', 'expert'), [(source * sourc...  2.72 us
    ppermute x1, starting transfers between devices, shards(): incoming = lax.ppermute(upstream[0], 'pipe', earlier_section)  2.46 us
    pallas_call x1, Pallas kernels, shards(): call(functools.partial(first_kernel, [0, half]), [shape(capacity, width)...  1.78 us
    pallas_call x1, Pallas kernels, shards(): call(functools.partial(last_kernel, others, half - 1), [shape(capacity, w...  1.69 us
  transfers between devices with their start and end apart: 15, of which 10 were waited for; matrix products, arithmetic and copies ran while one was open for 1% of the time, Pallas kernels for 6%

profile of v3, /device:TPU:0, one launch (start us, length us, event | category | flops | bytes accessed | tf_op | source)
XLA Modules:
  0.0 70.9 jit_solution(15233933736871963658)
XLA Ops:
  0.6 2.5 %collective-permute-start = (bf16[128,2048]{1,0:T(8,128)(2,1)}, bf16[128,2048]{1,0:T(8,128)(2,1)S(1)}, u32[]{:S(2)}, u32[]{:S(2)}) collective-permute-start(bf16[128,2048]{1,0:T(8,128)(2,1)} %bitcast.36), channel_id=1, source_target_pairs={{0,24},{8,0},{16,8},{24,16},{1,25},{9,1},{17,9},{25,17},{2,26},{10... | collective-permute-start | bytes 1572872 | tf_op jit(solution)/shard_map/ppermute | solution.py:243
  3.1 1.0 %slice_bitcast_fusion = bf16[128,1280]{1,0:T(8,128)(2,1)S(1)} fusion(bf16[1,128,2048]{2,1,0:T(8,128)(2,1)} %param.8), kind=kLoop, calls=%fused_computation | loop fusion | bytes 655360 | tf_op jit(solution)/shard_map/squeeze | solution.py:235
  4.1 2.7 %collective-permute-start.2 = (bf16[128,1280]{1,0:T(8,128)(2,1)S(1)}, bf16[128,1280]{1,0:T(8,128)(2,1)S(1)}, u32[]{:S(2)}, u32[]{:S(2)}) collective-permute-start(bf16[128,1280]{1,0:T(8,128)(2,1)S(1)} %slice_bitcast_fusion), channel_id=1, source_target_pairs={{0,28},{2,30},{4,24},{6,26},{8,4},{10,6},{12,0},{14,2},{16,12},{18... | collective-permute-start | bytes 983048 | tf_op jit(solution)/shard_map/ppermute | solution.py:234
  6.9 1.0 %copy-done.7 = bf16[1,128,2048]{2,1,0:T(8,128)(2,1)S(1)} copy-done((bf16[1,128,2048]{2,1,0:T(8,128)(2,1)S(1)}, bf16[1,128,2048]{2,1,0:T(8,128)(2,1)}, u32[]{:S(2)}) %copy-start.7) | copy-done | bytes 524312
  7.9 0.7 %copy-done.9 = bf16[1,2048,4]{1,2,0:T(4,128)(2,1)S(1)} copy-done((bf16[1,2048,4]{1,2,0:T(4,128)(2,1)S(1)}, bf16[1,2048,4]{1,2,0:T(4,128)(2,1)}, u32[]{:S(2)}) %copy-start.9) | copy-done | bytes 16408
  8.6 0.7 copy-done.11
  9.3 0.3 shard_map.95.meta_ref.refs_0_
  9.6 0.8 %collective-permute-done.incoming_ref = bf16[128,2048]{1,0:T(8,128)(2,1)S(1)} collective-permute-done((bf16[128,2048]{1,0:T(8,128)(2,1)}, bf16[128,2048]{1,0:T(8,128)(2,1)S(1)}, u32[]{:S(2)}, u32[]{:S(2)}) %collective-permute-start) | collective-permute-done | bytes 524320 | tf_op jit(solution)/shard_map/ppermute | solution.py:243
  10.4 0.4 shard_map.96
  10.7 3.5 %collective-permute-start.4 = (bf16[72,2048]{1,0:T(8,128)(2,1)S(1)}, bf16[72,2048]{1,0:T(8,128)(2,1)S(1)}, u32[]{:S(2)}, u32[]{:S(2)}) collective-permute-start(bf16[72,2048]{1,0:T(8,128)(2,1)S(1)} %get-tuple-element.17), channel_id=1, source_target_pairs={{0,2},{2,0},{4,6},{6,4},{1,3},{3,1},{5,7},{7,5},{8,10},{10,8},{12,... | collective-permute-start | bytes 884744 | tf_op jit(solution)/shard_map/ppermute | solution.py:32
  14.2 1.1 %collective-permute-start.1 = (f32[8,128]{1,0:T(8,128)S(1)}, f32[8,128]{1,0:T(8,128)S(1)}, u32[]{:S(2)}, u32[]{:S(2)}) collective-permute-start(f32[8,128]{1,0:T(8,128)S(1)} %shard_map.95.meta_ref.refs_0_), channel_id=1, source_target_pairs={{0,4},{2,6},{4,0},{6,2},{1,5},{3,7},{5,1},{7,3},{8,12},{10,14},{12... | collective-permute-start | bytes 12296 | tf_op jit(solution)/shard_map/ppermute | solution.py:32
  15.3 1.8 %collective-permute-start.3 = (bf16[72,768]{1,0:T(8,128)(2,1)S(1)}, bf16[72,768]{1,0:T(8,128)(2,1)S(1)}, u32[]{:S(2)}, u32[]{:S(2)}) collective-permute-start(bf16[72,768]{1,0:T(8,128)(2,1)S(1)} %get-tuple-element.14), channel_id=1, source_target_pairs={{0,4},{2,6},{4,0},{6,2},{1,5},{3,7},{5,1},{7,3},{8,12},{10,14},{12... | collective-permute-start | bytes 331784 | tf_op jit(solution)/shard_map/ppermute | solution.py:32
  17.2 1.5 %copy-done = bf16[1,1,448,2048]{3,2,1,0:T(8,128)(2,1)S(1)} copy-done((bf16[1,1,448,2048]{3,2,1,0:T(8,128)(2,1)S(1)}, bf16[1,1,448,2048]{3,2,1,0:T(8,128)(2,1)}, u32[]{:S(2)}) %copy-start) | copy-done | bytes 1835032
  18.7 1.5 %copy-done.2 = bf16[1,1,448,2048]{3,2,1,0:T(8,128)(2,1)S(1)} copy-done((bf16[1,1,448,2048]{3,2,1,0:T(8,128)(2,1)S(1)}, bf16[1,1,448,2048]{3,2,1,0:T(8,128)(2,1)}, u32[]{:S(2)}) %copy-start.2) | copy-done | bytes 1835032
  20.2 1.5 %copy-done.4 = bf16[1,1,448,2048]{3,2,1,0:T(8,128)(2,1)S(1)} copy-done((bf16[1,1,448,2048]{3,2,1,0:T(8,128)(2,1)S(1)}, bf16[1,1,448,2048]{3,2,1,0:T(8,128)(2,1)}, u32[]{:S(2)}) %copy-start.4) | copy-done | bytes 1835032
  21.7 1.2 %collective-permute-done.1.meta_ref = f32[8,128]{1,0:T(8,128)S(1)} collective-permute-done((f32[8,128]{1,0:T(8,128)S(1)}, f32[8,128]{1,0:T(8,128)S(1)}, u32[]{:S(2)}, u32[]{:S(2)}) %collective-permute-start.1) | collective-permute-done | bytes 4128 | tf_op jit(solution)/shard_map/ppermute | solution.py:32
  22.9 0.0 collective-permute-done.2.raw_ref._raw
  22.9 0.2 shard_map.99
  23.1 2.1 %collective-permute-start.5 = (bf16[72,1280]{1,0:T(8,128)(2,1)S(1)}, bf16[72,1280]{1,0:T(8,128)(2,1)S(1)}, u32[]{:S(2)}, u32[]{:S(2)}) collective-permute-start(bf16[72,1280]{1,0:T(8,128)(2,1)S(1)} %shard_map.99), channel_id=1, source_target_pairs={{0,2},{2,0},{4,6},{6,4},{1,3},{3,1},{5,7},{7,5},{8,10},{10,8},{12,... | collective-permute-start | bytes 552968 | tf_op jit(solution)/shard_map/ppermute | solution.py:32
  25.2 0.2 shard_map.100
  25.4 0.0 copy-start.3
  25.4 0.0 copy-start.5
  25.4 1.4 %collective-permute-start.6 = (bf16[72,768]{1,0:T(8,128)(2,1)S(1)}, bf16[72,768]{1,0:T(8,128)(2,1)S(1)}, u32[]{:S(2)}, u32[]{:S(2)}) collective-permute-start(bf16[72,768]{1,0:T(8,128)(2,1)S(1)} %shard_map.100), channel_id=1, source_target_pairs={{0,6},{2,4},{4,2},{6,0},{1,7},{3,5},{5,3},{7,1},{8,14},{10,12},{12... | collective-permute-start | bytes 331784 | tf_op jit(solution)/shard_map/ppermute | solution.py:32
  26.9 0.0 collective-permute-done.3.tail_ref
  26.9 1.8 %shard_map.97 = (bf16[72,2176]{1,0:T(8,128)(2,1)S(1)}, bf16[72,2176]{1,0:T(8,128)(2,1)S(1)}) custom-call(s32[1]{0:T(128)} %bitcast.me_ref, bf16[4,72,896]{2,1,0:T(8,128)(2,1)S(1)} %bitcast.29, bf16[448,2048]{1,0:T(8,128)(2,1)S(1)} %bitcast.20, bf16[448,2048]{1,0:T(8,128)(2,1)S(1)} %bitcast.23, bf16[448,2048]{1,0:T(8,128)(2,1)S(1)} %bitcast.26, ...), custom_call_target="tpu_custom_call" | custom-call | flops 792723456 | bytes 6684672 | tf_op jit(solution)/shard_map/pallas_call | solution.py:299
  28.7 0.5 collective-permute-start.8
  29.2 5.4 %collective-permute-done.6.refs_2_ = bf16[72,768]{1,0:T(8,128)(2,1)S(1)} collective-permute-done((bf16[72,768]{1,0:T(8,128)(2,1)S(1)}, bf16[72,768]{1,0:T(8,128)(2,1)S(1)}, u32[]{:S(2)}, u32[]{:S(2)}) %collective-permute-start.6) | collective-permute-done | bytes 110624 | tf_op jit(solution)/shard_map/ppermute | solution.py:32
  34.6 1.8 %collective-permute-done.5.refs_1_ = bf16[72,1280]{1,0:T(8,128)(2,1)S(1)} collective-permute-done((bf16[72,1280]{1,0:T(8,128)(2,1)S(1)}, bf16[72,1280]{1,0:T(8,128)(2,1)S(1)}, u32[]{:S(2)}, u32[]{:S(2)}) %collective-permute-start.5) | collective-permute-done | bytes 184352 | tf_op jit(solution)/shard_map/ppermute | solution.py:32
  36.4 0.0 collective-permute-done.4.refs_0_
  36.4 0.0 copy-start.8
  36.4 0.0 copy-start.10
  36.5 1.7 %shard_map.101 = (bf16[72,2064]{1,0:T(8,128)(2,1)S(1)}, bf16[72,1024]{1,0:T(8,128)(2,1)S(1)}, bf16[72,1152]{1,0:T(8,128)(2,1)S(1)}) custom-call(s32[1]{0:T(128)} %bitcast.me_ref, bf16[4,72,896]{2,1,0:T(8,128)(2,1)S(1)} %bitcast.30, bf16[448,2048]{1,0:T(8,128)(2,1)S(1)} %bitcast.21, bf16[448,2048]{1,0:T(8,128)(2,1)S(1)} %bitcast.24, ...), custom_call_target="tpu_custom_call" | custom-call | flops 792723456 | bytes 6684672 | tf_op jit(solution)/shard_map/pallas_call | solution.py:307
  38.1 0.1 collective-permute-start.7
  38.2 3.6 %collective-permute-start.9 = (bf16[72,1024]{1,0:T(8,128)(2,1)S(1)}, bf16[72,1024]{1,0:T(8,128)(2,1)S(1)}, u32[]{:S(2)}, u32[]{:S(2)}) collective-permute-start(bf16[72,1024]{1,0:T(8,128)(2,1)S(1)} %get-tuple-element.20), channel_id=1, source_target_pairs={{0,6},{2,4},{4,2},{6,0},{1,7},{3,5},{5,3},{7,1},{8,14},{10,12},{12... | collective-permute-start | bytes 442376 | tf_op jit(solution)/shard_map/ppermute | solution.py:32
  41.8 5.9 %collective-permute-done.8.refs_2_ = bf16[72,2176]{1,0:T(8,128)(2,1)S(1)} collective-permute-done((bf16[72,2176]{1,0:T(8,128)(2,1)S(1)}, bf16[72,2176]{1,0:T(8,128)(2,1)S(1)}, u32[]{:S(2)}, u32[]{:S(2)}) %collective-permute-start.8) | collective-permute-done | bytes 313376 | tf_op jit(solution)/shard_map/ppermute | solution.py:32
  47.7 5.5 %collective-permute-done.9.refs_3_ = bf16[72,1024]{1,0:T(8,128)(2,1)S(1)} collective-permute-done((bf16[72,1024]{1,0:T(8,128)(2,1)S(1)}, bf16[72,1024]{1,0:T(8,128)(2,1)S(1)}, u32[]{:S(2)}, u32[]{:S(2)}) %collective-permute-start.9) | collective-permute-done | bytes 147488 | tf_op jit(solution)/shard_map/ppermute | solution.py:32
  53.2 4.3 %collective-permute-done.7.refs_1_ = bf16[72,2064]{1,0:T(8,128)(2,1)S(1)} collective-permute-done((bf16[72,2064]{1,0:T(8,128)(2,1)S(1)}, bf16[72,2064]{1,0:T(8,128)(2,1)S(1)}, u32[]{:S(2)}, u32[]{:S(2)}) %collective-permute-start.7) | collective-permute-done | bytes 297248 | tf_op jit(solution)/shard_map/ppermute | solution.py:32
  57.5 0.9 %shard_map.102 = (f32[4,2048]{1,0:T(4,128)S(1)}, f32[128,2048]{1,0:T(8,128)S(1)}) custom-call(f32[8,128]{1,0:T(8,128)S(1)} %shard_map.95.meta_ref.refs_0_, bf16[128,2048]{1,0:T(8,128)(2,1)S(1)} %bitcast.32, bf16[128,2048]{1,0:T(8,128)(2,1)S(1)} %collective-permute-done.incoming_ref, bf16[4,2048]{1,0:T(4,128)(2,1)S(1)} %bitcast.34, ...), custom_call_target="tpu_custom_call" | custom-call | flops 150994944 | bytes 3276800 | tf_op jit(solution)/shard_map/pallas_call | solution.py:316
  58.4 1.6 %collective-permute-start.11 = (f32[4,2048]{1,0:T(4,128)S(1)}, f32[4,2048]{1,0:T(4,128)S(1)}, u32[]{:S(2)}, u32[]{:S(2)}) collective-permute-start(f32[4,2048]{1,0:T(4,128)S(1)} %get-tuple-element.23), channel_id=1, source_target_pairs={{0,1},{1,0},{2,3},{3,2},{4,5},{5,4},{6,7},{7,6},{8,9},{9,8},{10,11... | collective-permute-start | bytes 98312 | tf_op jit(solution)/shard_map/ppermute | solution.py:32
  60.0 2.5 %collective-permute-start.10 = (bf16[72,1152]{1,0:T(8,128)(2,1)S(1)}, bf16[72,1152]{1,0:T(8,128)(2,1)S(1)}, u32[]{:S(2)}, u32[]{:S(2)}) collective-permute-start(bf16[72,1152]{1,0:T(8,128)(2,1)S(1)} %get-tuple-element.22), channel_id=1, source_target_pairs={{0,6},{2,4},{4,2},{6,0},{1,7},{3,5},{5,3},{7,1},{8,14},{10,12},{12... | collective-permute-start | bytes 497672 | tf_op jit(solution)/shard_map/ppermute | solution.py:32
  62.4 0.0 collective-permute-done.11
  62.5 2.5 %collective-permute-start.14 = (bf16[4,2048]{1,0:T(4,128)(2,1)S(1)}, bf16[4,2048]{1,0:T(4,128)(2,1)S(1)}, u32[]{:S(2)}, u32[]{:S(2)}) collective-permute-start(bf16[4,2048]{1,0:T(4,128)(2,1)S(1)} %get-tuple-element.26), channel_id=1, source_target_pairs={{0,6},{2,4},{4,2},{6,0},{1,7},{3,5},{5,3},{7,1},{8,14},{10,12},{12... | collective-permute-start | bytes 49160 | tf_op jit(solution)/shard_map/ppermute | solution.py:32
  64.9 0.0 collective-permute-start.13
  64.9 2.0 %collective-permute-start.12 = (bf16[4,2048]{1,0:T(4,128)(2,1)S(1)}, bf16[4,2048]{1,0:T(4,128)(2,1)S(1)}, u32[]{:S(2)}, u32[]{:S(2)}) collective-permute-start(bf16[4,2048]{1,0:T(4,128)(2,1)S(1)} %get-tuple-element.26), channel_id=1, source_target_pairs={{0,2},{2,0},{4,6},{6,4},{1,3},{3,1},{5,7},{7,5},{8,10},{10,8},{12,... | collective-permute-start | bytes 49160 | tf_op jit(solution)/shard_map/ppermute | solution.py:32
  66.9 1.3 %collective-permute-done.10.refs_0_ = bf16[72,1152]{1,0:T(8,128)(2,1)S(1)} collective-permute-done((bf16[72,1152]{1,0:T(8,128)(2,1)S(1)}, bf16[72,1152]{1,0:T(8,128)(2,1)S(1)}, u32[]{:S(2)}, u32[]{:S(2)}) %collective-permute-start.10) | collective-permute-done | bytes 165920 | tf_op jit(solution)/shard_map/ppermute | solution.py:32
  68.2 0.2 collective-permute-done.14.refs_4_
  68.3 1.5 %collective-permute-done.13.refs_3_ = bf16[4,2048]{1,0:T(4,128)(2,1)S(1)} collective-permute-done((bf16[4,2048]{1,0:T(4,128)(2,1)S(1)}, bf16[4,2048]{1,0:T(4,128)(2,1)S(1)}, u32[]{:S(2)}, u32[]{:S(2)}) %collective-permute-start.13) | collective-permute-done | bytes 16416 | tf_op jit(solution)/shard_map/ppermute | solution.py:32
  69.8 1.1 %shard_map.103 = (bf16[128,2048]{1,0:T(8,128)(2,1)}, f32[4,2048]{1,0:T(4,128)}) custom-call(f32[8,128]{1,0:T(8,128)S(1)} %shard_map.95.meta_ref.refs_0_, f32[128,2048]{1,0:T(8,128)S(1)} %get-tuple-element.21.base_ref, bf16[72,1152]{1,0:T(8,128)(2,1)S(1)} %collective-permute-done.10.refs_0_, f32[4,2048]{1,0:T(4,128)S(1)} %get-tuple-element.27.refs_1_, ...), custom_call_target="tpu_custom_call" | custom-call | flops 37748736 | bytes 1867776 | tf_op jit(solution)/shard_map/pallas_call | solution.py:333
  (17 shorter events, 0.0 us)
Async XLA Ops:
  0.6 16.5 %copy-start.6 = (bf16[1,1,288,896]{3,2,1,0:T(8,128)(2,1)S(1)}, bf16[1,1,288,896]{3,2,1,0:T(8,128)(2,1)}, u32[]{:S(2)}) copy-start(bf16[1,1,288,896]{3,2,1,0:T(8,128)(2,1)} %param.15) | copy-start | bytes 1548292
  0.6 9.7 %collective-permute-start = (bf16[128,2048]{1,0:T(8,128)(2,1)}, bf16[128,2048]{1,0:T(8,128)(2,1)S(1)}, u32[]{:S(2)}, u32[]{:S(2)}) collective-permute-start(bf16[128,2048]{1,0:T(8,128)(2,1)} %bitcast.36), channel_id=1, source_target_pairs={{0,24},{8,0},{16,8},{24,16},{1,25},{9,1},{17,9},{25,17},{2,26},{10... | collective-permute-start | bytes 1572872 | tf_op jit(solution)/shard_map/ppermute | solution.py:243
  4.1 18.8 %collective-permute-start.2 = (bf16[128,1280]{1,0:T(8,128)(2,1)S(1)}, bf16[128,1280]{1,0:T(8,128)(2,1)S(1)}, u32[]{:S(2)}, u32[]{:S(2)}) collective-permute-start(bf16[128,1280]{1,0:T(8,128)(2,1)S(1)} %slice_bitcast_fusion), channel_id=1, source_target_pairs={{0,28},{2,30},{4,24},{6,26},{8,4},{10,6},{12,0},{14,2},{16,12},{18... | collective-permute-start | bytes 983048 | tf_op jit(solution)/shard_map/ppermute | solution.py:234
  6.8 1.0 %copy-start.7 = (bf16[1,128,2048]{2,1,0:T(8,128)(2,1)S(1)}, bf16[1,128,2048]{2,1,0:T(8,128)(2,1)}, u32[]{:S(2)}) copy-start(bf16[1,128,2048]{2,1,0:T(8,128)(2,1)} %param.9) | copy-start | bytes 1572868
  7.9 0.7 %copy-start.9 = (bf16[1,2048,4]{1,2,0:T(4,128)(2,1)S(1)}, bf16[1,2048,4]{1,2,0:T(4,128)(2,1)}, u32[]{:S(2)}) copy-start(bf16[1,2048,4]{1,2,0:T(4,128)(2,1)} %param.11) | copy-start | bytes 49156
  8.6 0.7 copy-start.11
  10.7 25.7 %collective-permute-start.4 = (bf16[72,2048]{1,0:T(8,128)(2,1)S(1)}, bf16[72,2048]{1,0:T(8,128)(2,1)S(1)}, u32[]{:S(2)}, u32[]{:S(2)}) collective-permute-start(bf16[72,2048]{1,0:T(8,128)(2,1)S(1)} %get-tuple-element.17), channel_id=1, source_target_pairs={{0,2},{2,0},{4,6},{6,4},{1,3},{3,1},{5,7},{7,5},{8,10},{10,8},{12,... | collective-permute-start | bytes 884744 | tf_op jit(solution)/shard_map/ppermute | solution.py:32
  14.2 8.7 %collective-permute-start.1 = (f32[8,128]{1,0:T(8,128)S(1)}, f32[8,128]{1,0:T(8,128)S(1)}, u32[]{:S(2)}, u32[]{:S(2)}) collective-permute-start(f32[8,128]{1,0:T(8,128)S(1)} %shard_map.95.meta_ref.refs_0_), channel_id=1, source_target_pairs={{0,4},{2,6},{4,0},{6,2},{1,5},{3,7},{5,1},{7,3},{8,12},{10,14},{12... | collective-permute-start | bytes 12296 | tf_op jit(solution)/shard_map/ppermute | solution.py:32
  15.3 11.5 %collective-permute-start.3 = (bf16[72,768]{1,0:T(8,128)(2,1)S(1)}, bf16[72,768]{1,0:T(8,128)(2,1)S(1)}, u32[]{:S(2)}, u32[]{:S(2)}) collective-permute-start(bf16[72,768]{1,0:T(8,128)(2,1)S(1)} %get-tuple-element.14), channel_id=1, source_target_pairs={{0,4},{2,6},{4,0},{6,2},{1,5},{3,7},{5,1},{7,3},{8,12},{10,14},{12... | collective-permute-start | bytes 331784 | tf_op jit(solution)/shard_map/ppermute | solution.py:32
  17.2 1.5 %copy-start = (bf16[1,1,448,2048]{3,2,1,0:T(8,128)(2,1)S(1)}, bf16[1,1,448,2048]{3,2,1,0:T(8,128)(2,1)}, u32[]{:S(2)}) copy-start(bf16[1,1,448,2048]{3,2,1,0:T(8,128)(2,1)} %param.12) | copy-start | bytes 5505028
  18.7 1.5 %copy-start.2 = (bf16[1,1,448,2048]{3,2,1,0:T(8,128)(2,1)S(1)}, bf16[1,1,448,2048]{3,2,1,0:T(8,128)(2,1)}, u32[]{:S(2)}) copy-start(bf16[1,1,448,2048]{3,2,1,0:T(8,128)(2,1)} %param.13) | copy-start | bytes 5505028
  20.2 1.5 %copy-start.4 = (bf16[1,1,448,2048]{3,2,1,0:T(8,128)(2,1)S(1)}, bf16[1,1,448,2048]{3,2,1,0:T(8,128)(2,1)}, u32[]{:S(2)}) copy-start(bf16[1,1,448,2048]{3,2,1,0:T(8,128)(2,1)} %param.14) | copy-start | bytes 5505028
  21.7 5.2 %copy-start.1 = (bf16[1,1,448,2048]{3,2,1,0:T(8,128)(2,1)S(1)}, bf16[1,1,448,2048]{3,2,1,0:T(8,128)(2,1)}, u32[]{:S(2)}) copy-start(bf16[1,1,448,2048]{3,2,1,0:T(8,128)(2,1)} %param.12) | copy-start | bytes 5505028
  23.1 13.3 %collective-permute-start.5 = (bf16[72,1280]{1,0:T(8,128)(2,1)S(1)}, bf16[72,1280]{1,0:T(8,128)(2,1)S(1)}, u32[]{:S(2)}, u32[]{:S(2)}) collective-permute-start(bf16[72,1280]{1,0:T(8,128)(2,1)S(1)} %shard_map.99), channel_id=1, source_target_pairs={{0,2},{2,0},{4,6},{6,4},{1,3},{3,1},{5,7},{7,5},{8,10},{10,8},{12,... | collective-permute-start | bytes 552968 | tf_op jit(solution)/shard_map/ppermute | solution.py:32
  25.4 11.0 %copy-start.3 = (bf16[1,1,448,2048]{3,2,1,0:T(8,128)(2,1)S(1)}, bf16[1,1,448,2048]{3,2,1,0:T(8,128)(2,1)}, u32[]{:S(2)}) copy-start(bf16[1,1,448,2048]{3,2,1,0:T(8,128)(2,1)} %param.13) | copy-start | bytes 5505028
  25.4 11.0 %copy-start.5 = (bf16[1,1,448,2048]{3,2,1,0:T(8,128)(2,1)S(1)}, bf16[1,1,448,2048]{3,2,1,0:T(8,128)(2,1)}, u32[]{:S(2)}) copy-start(bf16[1,1,448,2048]{3,2,1,0:T(8,128)(2,1)} %param.14) | copy-start | bytes 5505028
  25.4 9.1 %collective-permute-start.6 = (bf16[72,768]{1,0:T(8,128)(2,1)S(1)}, bf16[72,768]{1,0:T(8,128)(2,1)S(1)}, u32[]{:S(2)}, u32[]{:S(2)}) collective-permute-start(bf16[72,768]{1,0:T(8,128)(2,1)S(1)} %shard_map.100), channel_id=1, source_target_pairs={{0,6},{2,4},{4,2},{6,0},{1,7},{3,5},{5,3},{7,1},{8,14},{10,12},{12... | collective-permute-start | bytes 331784 | tf_op jit(solution)/shard_map/ppermute | solution.py:32
  28.7 19.0 %collective-permute-start.8 = (bf16[72,2176]{1,0:T(8,128)(2,1)S(1)}, bf16[72,2176]{1,0:T(8,128)(2,1)S(1)}, u32[]{:S(2)}, u32[]{:S(2)}) collective-permute-start(bf16[72,2176]{1,0:T(8,128)(2,1)S(1)} %get-tuple-element.19), channel_id=1, source_target_pairs={{0,4},{2,6},{4,0},{6,2},{1,5},{3,7},{5,1},{7,3},{8,12},{10,14},{12... | collective-permute-start | bytes 940040 | tf_op jit(solution)/shard_map/ppermute | solution.py:32
  36.4 21.0 %copy-start.8 = (bf16[1,128,2048]{2,1,0:T(8,128)(2,1)S(1)}, bf16[1,128,2048]{2,1,0:T(8,128)(2,1)}, u32[]{:S(2)}) copy-start(bf16[1,128,2048]{2,1,0:T(8,128)(2,1)} %param.9) | copy-start | bytes 1572868
  36.4 21.0 %copy-start.10 = (bf16[1,2048,4]{1,2,0:T(4,128)(2,1)S(1)}, bf16[1,2048,4]{1,2,0:T(4,128)(2,1)}, u32[]{:S(2)}) copy-start(bf16[1,2048,4]{1,2,0:T(4,128)(2,1)} %param.11) | copy-start | bytes 49156
  38.1 19.3 %collective-permute-start.7 = (bf16[72,2064]{1,0:T(8,128)(2,1)S(1)}, bf16[72,2064]{1,0:T(8,128)(2,1)S(1)}, u32[]{:S(2)}, u32[]{:S(2)}) collective-permute-start(bf16[72,2064]{1,0:T(8,128)(2,1)S(1)} %get-tuple-element.18), channel_id=1, source_target_pairs={{0,2},{2,0},{4,6},{6,4},{1,3},{3,1},{5,7},{7,5},{8,10},{10,8},{12,... | collective-permute-start | bytes 891656 | tf_op jit(solution)/shard_map/ppermute | solution.py:32
  38.2 14.9 %collective-permute-start.9 = (bf16[72,1024]{1,0:T(8,128)(2,1)S(1)}, bf16[72,1024]{1,0:T(8,128)(2,1)S(1)}, u32[]{:S(2)}, u32[]{:S(2)}) collective-permute-start(bf16[72,1024]{1,0:T(8,128)(2,1)S(1)} %get-tuple-element.20), channel_id=1, source_target_pairs={{0,6},{2,4},{4,2},{6,0},{1,7},{3,5},{5,3},{7,1},{8,14},{10,12},{12... | collective-permute-start | bytes 442376 | tf_op jit(solution)/shard_map/ppermute | solution.py:32
  58.4 4.0 %collective-permute-start.11 = (f32[4,2048]{1,0:T(4,128)S(1)}, f32[4,2048]{1,0:T(4,128)S(1)}, u32[]{:S(2)}, u32[]{:S(2)}) collective-permute-start(f32[4,2048]{1,0:T(4,128)S(1)} %get-tuple-element.23), channel_id=1, source_target_pairs={{0,1},{1,0},{2,3},{3,2},{4,5},{5,4},{6,7},{7,6},{8,9},{9,8},{10,11... | collective-permute-start | bytes 98312 | tf_op jit(solution)/shard_map/ppermute | solution.py:32
  60.0 8.2 %collective-permute-start.10 = (bf16[72,1152]{1,0:T(8,128)(2,1)S(1)}, bf16[72,1152]{1,0:T(8,128)(2,1)S(1)}, u32[]{:S(2)}, u32[]{:S(2)}) collective-permute-start(bf16[72,1152]{1,0:T(8,128)(2,1)S(1)} %get-tuple-element.22), channel_id=1, source_target_pairs={{0,6},{2,4},{4,2},{6,0},{1,7},{3,5},{5,3},{7,1},{8,14},{10,12},{12... | collective-permute-start | bytes 497672 | tf_op jit(solution)/shard_map/ppermute | solution.py:32
  62.5 5.9 %collective-permute-start.14 = (bf16[4,2048]{1,0:T(4,128)(2,1)S(1)}, bf16[4,2048]{1,0:T(4,128)(2,1)S(1)}, u32[]{:S(2)}, u32[]{:S(2)}) collective-permute-start(bf16[4,2048]{1,0:T(4,128)(2,1)S(1)} %get-tuple-element.26), channel_id=1, source_target_pairs={{0,6},{2,4},{4,2},{6,0},{1,7},{3,5},{5,3},{7,1},{8,14},{10,12},{12... | collective-permute-start | bytes 49160 | tf_op jit(solution)/shard_map/ppermute | solution.py:32
  64.9 4.9 %collective-permute-start.13 = (bf16[4,2048]{1,0:T(4,128)(2,1)S(1)}, bf16[4,2048]{1,0:T(4,128)(2,1)S(1)}, u32[]{:S(2)}, u32[]{:S(2)}) collective-permute-start(bf16[4,2048]{1,0:T(4,128)(2,1)S(1)} %get-tuple-element.26), channel_id=1, source_target_pairs={{0,4},{2,6},{4,0},{6,2},{1,5},{3,7},{5,1},{7,3},{8,12},{10,14},{12... | collective-permute-start | bytes 49160 | tf_op jit(solution)/shard_map/ppermute | solution.py:32
  64.9 4.9 %collective-permute-start.12 = (bf16[4,2048]{1,0:T(4,128)(2,1)S(1)}, bf16[4,2048]{1,0:T(4,128)(2,1)S(1)}, u32[]{:S(2)}, u32[]{:S(2)}) collective-permute-start(bf16[4,2048]{1,0:T(4,128)(2,1)S(1)} %get-tuple-element.26), channel_id=1, source_target_pairs={{0,2},{2,0},{4,6},{6,4},{1,3},{3,1},{5,7},{7,5},{8,10},{10,8},{12,... | collective-permute-start | bytes 49160 | tf_op jit(solution)/shard_map/ppermute | solution.py:32

commit v4 on v3

--- a/solution.py
+++ b/solution.py
@@ -219,7 +219,7 @@
     pre = saved_preacts[0, 0].reshape(sources, capacity, 2 * hidden)
     half = sources // 2
     split = features * 5 // 8
-    early = features * 7 // 16
+    early = features * 9 // 16
     near, last = list(range(half)), list(range(half + 1, sources))
 
     def shape(rows, columns, kind=BF16):
@@ -280,7 +280,6 @@
     tails_of_last = [exchanged(value, "expert", away) for away, value in zip(last, late)]
     relayed_heads = [exchanged(value, "expert", away - half) for away, value in zip(last, relays)]
 
-    others = near[1:] + last
 
     def widths_of(away):
         if away > half:
@@ -304,14 +303,20 @@
         weight_bytes + 4 * block_bytes,
     )(me, pre, gate, up, down, far_meta, raw, far_tail, rows[0])
     returned([0, half], first)
-    ends = call(
-        functools.partial(last_kernel, others, half - 1),
-        [shape(capacity, width) for away in others for width in widths_of(away)],
-        [SMEM] + [VMEM] * 4 + [ANY] + [VMEM] * (half - 1 + 2 * len(last)),
-        row_flops * len(others),
-        weight_bytes + 2 * block_bytes * len(others),
-    )(me, pre, gate, up, down, first[0], *rows[1:], *relayed_heads, *tails_of_last)
-    returned(others, ends)
+    before = first[0]
+    for aways, near_count, values in (
+        (near[1:], half - 1, rows[1:]),
+        (last, 0, relayed_heads + tails_of_last),
+    ):
+        ends = call(
+            functools.partial(last_kernel, aways, near_count),
+            [shape(capacity, width) for away in aways for width in widths_of(away)],
+            [SMEM] + [VMEM] * 4 + [ANY] + [VMEM] * len(values),
+            row_flops * len(aways),
+            weight_bytes + 2 * block_bytes * len(aways),
+        )(me, pre, gate, up, down, before, *values)
+        returned(aways, ends)
+        before = ends[0]
 
     partial, base = call(
         logit_kernel,

time: 71.3 us -> 68.1 us (0.955)
  waiting for transfers between devices: 27.9 us -> 18.4 us
  starting transfers between devices: 27.8 us -> 32.7 us
  Pallas kernels: 6.45 us -> 7.87 us
    ppermute x13, waiting for transfers between devices: 27.1 us -> 17.6 us  [exchanged(): lax.ppermute(value, axis, [(at, at ^ distance) for at in range(count)])]
    ppermute x13, starting transfers between devices: 22.6 us -> 27.5 us  [exchanged(): lax.ppermute(value, axis, [(at, at ^ distance) for at in range(count)])]
    pallas_call x1 -> x2, Pallas kernels: 1.69 us -> 3.11 us  [shards(): call(functools.partial(last_kernel, aways, near_count), [shape(capacity,...]
  transfers between devices with their start and end apart: 15 -> 15, of which waited for: 10 -> 7; matrix products, arithmetic and copies ran while one was open for 1% -> 2% of each run, Pallas kernels for 6% -> 9%
where the time goes in v4:
time: 68.1 us; the launch traced here: 67.7 us
  starting transfers between devices  32.7 us (48%)
  waiting for transfers between devices  18.4 us (27%)
  local copies, waits for them, and re-layouts  7.99 us (12%)
  Pallas kernels  7.87 us (12%)
  between operations  0.76 us (1%)
    ppermute x13, starting transfers between devices, exchanged(): lax.ppermute(value, axis, [(at, at ^ distance) for at in range(count)])  27.5 us
    ppermute x13, waiting for transfers between devices, exchanged(): lax.ppermute(value, axis, [(at, at ^ distance) for at in range(count)])  17.6 us
    unnamed x24, local copies, waits for them, and re-layouts  6.97 us
    pallas_call x2, Pallas kernels, shards(): call(functools.partial(last_kernel, aways, near_count), [shape(capacity,...  3.11 us
    ppermute x1, starting transfers between devices, shards(): lax.ppermute(upstream[0, :, :split], ('pipe', 'expert'), [(source * sourc...  2.72 us
    ppermute x1, starting transfers between devices, shards(): incoming = lax.ppermute(upstream[0], 'pipe', earlier_section)  2.46 us
    pallas_call x1, Pallas kernels, shards(): call(functools.partial(first_kernel, [0, half]), [shape(capacity, width)...  1.77 us
  transfers between devices with their start and end apart: 15, of which 7 were waited for; matrix products, arithmetic and copies ran while one was open for 2% of the time, Pallas kernels for 9%

profile of v4, /device:TPU:0, one launch (start us, length us, event | category | flops | bytes accessed | tf_op | source)
XLA Modules:
  0.0 67.7 jit_solution(16189649437907087915)
XLA Ops:
  0.6 2.5 %collective-permute-start = (bf16[128,2048]{1,0:T(8,128)(2,1)}, bf16[128,2048]{1,0:T(8,128)(2,1)S(1)}, u32[]{:S(2)}, u32[]{:S(2)}) collective-permute-start(bf16[128,2048]{1,0:T(8,128)(2,1)} %bitcast.40), channel_id=1, source_target_pairs={{0,24},{8,0},{16,8},{24,16},{1,25},{9,1},{17,9},{25,17},{2,26},{10... | collective-permute-start | bytes 1572872 | tf_op jit(solution)/shard_map/ppermute | solution.py:243
  3.1 1.0 %slice_bitcast_fusion = bf16[128,1280]{1,0:T(8,128)(2,1)S(1)} fusion(bf16[1,128,2048]{2,1,0:T(8,128)(2,1)} %param.8), kind=kLoop, calls=%fused_computation | loop fusion | bytes 655360 | tf_op jit(solution)/shard_map/squeeze | solution.py:235
  4.1 2.7 %collective-permute-start.2 = (bf16[128,1280]{1,0:T(8,128)(2,1)S(1)}, bf16[128,1280]{1,0:T(8,128)(2,1)S(1)}, u32[]{:S(2)}, u32[]{:S(2)}) collective-permute-start(bf16[128,1280]{1,0:T(8,128)(2,1)S(1)} %slice_bitcast_fusion), channel_id=1, source_target_pairs={{0,28},{2,30},{4,24},{6,26},{8,4},{10,6},{12,0},{14,2},{16,12},{18... | collective-permute-start | bytes 983048 | tf_op jit(solution)/shard_map/ppermute | solution.py:234
  6.9 1.0 %copy-done.7 = bf16[1,128,2048]{2,1,0:T(8,128)(2,1)S(1)} copy-done((bf16[1,128,2048]{2,1,0:T(8,128)(2,1)S(1)}, bf16[1,128,2048]{2,1,0:T(8,128)(2,1)}, u32[]{:S(2)}) %copy-start.7) | copy-done | bytes 524312
  7.9 0.7 %copy-done.9 = bf16[1,2048,4]{1,2,0:T(4,128)(2,1)S(1)} copy-done((bf16[1,2048,4]{1,2,0:T(4,128)(2,1)S(1)}, bf16[1,2048,4]{1,2,0:T(4,128)(2,1)}, u32[]{:S(2)}) %copy-start.9) | copy-done | bytes 16408
  8.6 0.7 copy-done.11
  9.3 0.3 shard_map.95.meta_ref.refs_0_
  9.6 0.8 %collective-permute-done.incoming_ref = bf16[128,2048]{1,0:T(8,128)(2,1)S(1)} collective-permute-done((bf16[128,2048]{1,0:T(8,128)(2,1)}, bf16[128,2048]{1,0:T(8,128)(2,1)S(1)}, u32[]{:S(2)}, u32[]{:S(2)}) %collective-permute-start) | collective-permute-done | bytes 524320 | tf_op jit(solution)/shard_map/ppermute | solution.py:243
  10.4 0.4 shard_map.96
  10.7 3.5 %collective-permute-start.4 = (bf16[72,2048]{1,0:T(8,128)(2,1)S(1)}, bf16[72,2048]{1,0:T(8,128)(2,1)S(1)}, u32[]{:S(2)}, u32[]{:S(2)}) collective-permute-start(bf16[72,2048]{1,0:T(8,128)(2,1)S(1)} %get-tuple-element.16), channel_id=1, source_target_pairs={{0,2},{2,0},{4,6},{6,4},{1,3},{3,1},{5,7},{7,5},{8,10},{10,8},{12,... | collective-permute-start | bytes 884744 | tf_op jit(solution)/shard_map/ppermute | solution.py:32
  14.2 1.1 %collective-permute-start.3 = (bf16[72,768]{1,0:T(8,128)(2,1)S(1)}, bf16[72,768]{1,0:T(8,128)(2,1)S(1)}, u32[]{:S(2)}, u32[]{:S(2)}) collective-permute-start(bf16[72,768]{1,0:T(8,128)(2,1)S(1)} %get-tuple-element.13), channel_id=1, source_target_pairs={{0,4},{2,6},{4,0},{6,2},{1,5},{3,7},{5,1},{7,3},{8,12},{10,14},{12... | collective-permute-start | bytes 331784 | tf_op jit(solution)/shard_map/ppermute | solution.py:32
  15.3 1.8 %collective-permute-start.1 = (f32[8,128]{1,0:T(8,128)S(1)}, f32[8,128]{1,0:T(8,128)S(1)}, u32[]{:S(2)}, u32[]{:S(2)}) collective-permute-start(f32[8,128]{1,0:T(8,128)S(1)} %shard_map.95.meta_ref.refs_0_), channel_id=1, source_target_pairs={{0,4},{2,6},{4,0},{6,2},{1,5},{3,7},{5,1},{7,3},{8,12},{10,14},{12... | collective-permute-start | bytes 12296 | tf_op jit(solution)/shard_map/ppermute | solution.py:32
  17.2 1.5 %copy-done = bf16[1,1,448,2048]{3,2,1,0:T(8,128)(2,1)S(1)} copy-done((bf16[1,1,448,2048]{3,2,1,0:T(8,128)(2,1)S(1)}, bf16[1,1,448,2048]{3,2,1,0:T(8,128)(2,1)}, u32[]{:S(2)}) %copy-start) | copy-done | bytes 1835032
  18.7 1.5 %copy-done.2 = bf16[1,1,448,2048]{3,2,1,0:T(8,128)(2,1)S(1)} copy-done((bf16[1,1,448,2048]{3,2,1,0:T(8,128)(2,1)S(1)}, bf16[1,1,448,2048]{3,2,1,0:T(8,128)(2,1)}, u32[]{:S(2)}) %copy-start.2) | copy-done | bytes 1835032
  20.2 1.5 %copy-done.4 = bf16[1,1,448,2048]{3,2,1,0:T(8,128)(2,1)S(1)} copy-done((bf16[1,1,448,2048]{3,2,1,0:T(8,128)(2,1)S(1)}, bf16[1,1,448,2048]{3,2,1,0:T(8,128)(2,1)}, u32[]{:S(2)}) %copy-start.4) | copy-done | bytes 1835032
  21.7 0.0 collective-permute-done.2.raw_ref._raw
  21.7 0.2 shard_map.101
  21.9 4.0 %collective-permute-start.8 = (bf16[72,768]{1,0:T(8,128)(2,1)S(1)}, bf16[72,768]{1,0:T(8,128)(2,1)S(1)}, u32[]{:S(2)}, u32[]{:S(2)}) collective-permute-start(bf16[72,768]{1,0:T(8,128)(2,1)S(1)} %shard_map.101), channel_id=1, source_target_pairs={{0,6},{2,4},{4,2},{6,0},{1,7},{3,5},{5,3},{7,1},{8,14},{10,12},{12... | collective-permute-start | bytes 331784 | tf_op jit(solution)/shard_map/ppermute | solution.py:32
  25.9 0.0 collective-permute-done.1.meta_ref
  25.9 0.2 shard_map.100
  26.1 0.0 copy-start.3
  26.1 0.0 copy-start.5
  26.1 2.0 %collective-permute-start.7 = (bf16[72,1280]{1,0:T(8,128)(2,1)S(1)}, bf16[72,1280]{1,0:T(8,128)(2,1)S(1)}, u32[]{:S(2)}, u32[]{:S(2)}) collective-permute-start(bf16[72,1280]{1,0:T(8,128)(2,1)S(1)} %shard_map.100), channel_id=1, source_target_pairs={{0,2},{2,0},{4,6},{6,4},{1,3},{3,1},{5,7},{7,5},{8,10},{10,8},{12,... | collective-permute-start | bytes 552968 | tf_op jit(solution)/shard_map/ppermute | solution.py:32
  28.1 0.0 collective-permute-done.3.tail_ref
  28.2 1.8 %shard_map.97 = (bf16[72,2176]{1,0:T(8,128)(2,1)S(1)}, bf16[72,2176]{1,0:T(8,128)(2,1)S(1)}) custom-call(s32[1]{0:T(128)} %bitcast.me_ref, bf16[4,72,896]{2,1,0:T(8,128)(2,1)S(1)} %bitcast.32, bf16[448,2048]{1,0:T(8,128)(2,1)S(1)} %bitcast.20, bf16[448,2048]{1,0:T(8,128)(2,1)S(1)} %bitcast.24, bf16[448,2048]{1,0:T(8,128)(2,1)S(1)} %bitcast.28, ...), custom_call_target="tpu_custom_call" | custom-call | flops 792723456 | bytes 6684672 | tf_op jit(solution)/shard_map/pallas_call | solution.py:298
  29.9 3.4 %collective-permute-start.6 = (bf16[72,2176]{1,0:T(8,128)(2,1)S(1)}, bf16[72,2176]{1,0:T(8,128)(2,1)S(1)}, u32[]{:S(2)}, u32[]{:S(2)}) collective-permute-start(bf16[72,2176]{1,0:T(8,128)(2,1)S(1)} %get-tuple-element.17), channel_id=1, source_target_pairs={{0,4},{2,6},{4,0},{6,2},{1,5},{3,7},{5,1},{7,3},{8,12},{10,14},{12... | collective-permute-start | bytes 940040 | tf_op jit(solution)/shard_map/ppermute | solution.py:32
  33.4 0.0 collective-permute-done.4.refs_0_
  33.4 1.6 %shard_map.98._ = bf16[72,2064]{1,0:T(8,128)(2,1)S(1)} custom-call(s32[1]{0:T(128)} %bitcast.me_ref, bf16[4,72,896]{2,1,0:T(8,128)(2,1)S(1)} %bitcast.33, bf16[448,2048]{1,0:T(8,128)(2,1)S(1)} %bitcast.21, bf16[448,2048]{1,0:T(8,128)(2,1)S(1)} %bitcast.25, bf16[448,2048]{1,0:T(8,128)(2,1)S(1)} %bitcast.29, bf16[72,2176]{1,0:T(8,128)(2,1)S(1)} %get-tuple-element.15._.refs_0_, ...), custom_call_target="tpu_custom_call" | custom-call | flops 396361728 | bytes 6094848 | tf_op jit(solution)/shard_map/pallas_call | solution.py:311
  34.9 0.0 copy-start.8
  35.0 0.0 copy-start.10
  35.0 0.1 collective-permute-start.5
  35.1 3.1 %collective-permute-done.7.refs_0_ = bf16[72,1280]{1,0:T(8,128)(2,1)S(1)} collective-permute-done((bf16[72,1280]{1,0:T(8,128)(2,1)S(1)}, bf16[72,1280]{1,0:T(8,128)(2,1)S(1)}, u32[]{:S(2)}, u32[]{:S(2)}) %collective-permute-start.7) | collective-permute-done | bytes 184352 | tf_op jit(solution)/shard_map/ppermute | solution.py:32
  38.2 1.6 %shard_map.102 = (bf16[72,1280]{1,0:T(8,128)(2,1)S(1)}, bf16[72,896]{1,0:T(8,128)(2,1)S(1)}) custom-call(s32[1]{0:T(128)} %bitcast.me_ref, bf16[4,72,896]{2,1,0:T(8,128)(2,1)S(1)} %bitcast.34, bf16[448,2048]{1,0:T(8,128)(2,1)S(1)} %bitcast.22, bf16[448,2048]{1,0:T(8,128)(2,1)S(1)} %bitcast.26, bf16[448,2048]{1,0:T(8,128)(2,1)S(1)} %bitcast.30, ...), custom_call_target="tpu_custom_call" | custom-call | flops 396361728 | bytes 6094848 | tf_op jit(solution)/shard_map/pallas_call | solution.py:311
  39.8 2.9 %collective-permute-start.9 = (bf16[72,1280]{1,0:T(8,128)(2,1)S(1)}, bf16[72,1280]{1,0:T(8,128)(2,1)S(1)}, u32[]{:S(2)}, u32[]{:S(2)}) collective-permute-start(bf16[72,1280]{1,0:T(8,128)(2,1)S(1)} %get-tuple-element.18), channel_id=1, source_target_pairs={{0,6},{2,4},{4,2},{6,0},{1,7},{3,5},{5,3},{7,1},{8,14},{10,12},{12... | collective-permute-start | bytes 552968 | tf_op jit(solution)/shard_map/ppermute | solution.py:32
  42.6 5.8 %collective-permute-done.6.refs_2_ = bf16[72,2176]{1,0:T(8,128)(2,1)S(1)} collective-permute-done((bf16[72,2176]{1,0:T(8,128)(2,1)S(1)}, bf16[72,2176]{1,0:T(8,128)(2,1)S(1)}, u32[]{:S(2)}, u32[]{:S(2)}) %collective-permute-start.6) | collective-permute-done | bytes 313376 | tf_op jit(solution)/shard_map/ppermute | solution.py:32
  48.4 4.9 %collective-permute-done.9.refs_3_ = bf16[72,1280]{1,0:T(8,128)(2,1)S(1)} collective-permute-done((bf16[72,1280]{1,0:T(8,128)(2,1)S(1)}, bf16[72,1280]{1,0:T(8,128)(2,1)S(1)}, u32[]{:S(2)}, u32[]{:S(2)}) %collective-permute-start.9) | collective-permute-done | bytes 184352 | tf_op jit(solution)/shard_map/ppermute | solution.py:32
  53.3 0.8 %collective-permute-done.5.refs_1_ = bf16[72,2064]{1,0:T(8,128)(2,1)S(1)} collective-permute-done((bf16[72,2064]{1,0:T(8,128)(2,1)S(1)}, bf16[72,2064]{1,0:T(8,128)(2,1)S(1)}, u32[]{:S(2)}, u32[]{:S(2)}) %collective-permute-start.5) | collective-permute-done | bytes 297248 | tf_op jit(solution)/shard_map/ppermute | solution.py:32
  54.2 0.9 %shard_map.103 = (f32[4,2048]{1,0:T(4,128)S(1)}, f32[128,2048]{1,0:T(8,128)S(1)}) custom-call(f32[8,128]{1,0:T(8,128)S(1)} %shard_map.95.meta_ref.refs_0_, bf16[128,2048]{1,0:T(8,128)(2,1)S(1)} %bitcast.36, bf16[128,2048]{1,0:T(8,128)(2,1)S(1)} %collective-permute-done.incoming_ref, bf16[4,2048]{1,0:T(4,128)(2,1)S(1)} %bitcast.38, ...), custom_call_target="tpu_custom_call" | custom-call | flops 150994944 | bytes 3276800 | tf_op jit(solution)/shard_map/pallas_call | solution.py:321
  55.1 1.6 %collective-permute-start.11 = (f32[4,2048]{1,0:T(4,128)S(1)}, f32[4,2048]{1,0:T(4,128)S(1)}, u32[]{:S(2)}, u32[]{:S(2)}) collective-permute-start(f32[4,2048]{1,0:T(4,128)S(1)} %get-tuple-element.21), channel_id=1, source_target_pairs={{0,1},{1,0},{2,3},{3,2},{4,5},{5,4},{6,7},{7,6},{8,9},{9,8},{10,11... | collective-permute-start | bytes 98312 | tf_op jit(solution)/shard_map/ppermute | solution.py:32
  56.7 2.6 %collective-permute-start.10 = (bf16[72,896]{1,0:T(8,128)(2,1)S(1)}, bf16[72,896]{1,0:T(8,128)(2,1)S(1)}, u32[]{:S(2)}, u32[]{:S(2)}) collective-permute-start(bf16[72,896]{1,0:T(8,128)(2,1)S(1)} %get-tuple-element.20), channel_id=1, source_target_pairs={{0,6},{2,4},{4,2},{6,0},{1,7},{3,5},{5,3},{7,1},{8,14},{10,12},{12... | collective-permute-start | bytes 387080 | tf_op jit(solution)/shard_map/ppermute | solution.py:32
  59.3 2.6 %collective-permute-start.14 = (bf16[4,2048]{1,0:T(4,128)(2,1)S(1)}, bf16[4,2048]{1,0:T(4,128)(2,1)S(1)}, u32[]{:S(2)}, u32[]{:S(2)}) collective-permute-start(bf16[4,2048]{1,0:T(4,128)(2,1)S(1)} %get-tuple-element.24), channel_id=1, source_target_pairs={{0,6},{2,4},{4,2},{6,0},{1,7},{3,5},{5,3},{7,1},{8,14},{10,12},{12... | collective-permute-start | bytes 49160 | tf_op jit(solution)/shard_map/ppermute | solution.py:32
  61.9 0.5 collective-permute-start.13
  62.4 1.3 %collective-permute-start.12 = (bf16[4,2048]{1,0:T(4,128)(2,1)S(1)}, bf16[4,2048]{1,0:T(4,128)(2,1)S(1)}, u32[]{:S(2)}, u32[]{:S(2)}) collective-permute-start(bf16[4,2048]{1,0:T(4,128)(2,1)S(1)} %get-tuple-element.24), channel_id=1, source_target_pairs={{0,2},{2,0},{4,6},{6,4},{1,3},{3,1},{5,7},{7,5},{8,10},{10,8},{12,... | collective-permute-start | bytes 49160 | tf_op jit(solution)/shard_map/ppermute | solution.py:32
  63.7 0.0 collective-permute-done.10.refs_0_
  63.7 1.2 %collective-permute-done.14.refs_4_ = bf16[4,2048]{1,0:T(4,128)(2,1)S(1)} collective-permute-done((bf16[4,2048]{1,0:T(4,128)(2,1)S(1)}, bf16[4,2048]{1,0:T(4,128)(2,1)S(1)}, u32[]{:S(2)}, u32[]{:S(2)}) %collective-permute-start.14) | collective-permute-done | bytes 16416 | tf_op jit(solution)/shard_map/ppermute | solution.py:32
  64.9 1.8 %collective-permute-done.13.refs_3_ = bf16[4,2048]{1,0:T(4,128)(2,1)S(1)} collective-permute-done((bf16[4,2048]{1,0:T(4,128)(2,1)S(1)}, bf16[4,2048]{1,0:T(4,128)(2,1)S(1)}, u32[]{:S(2)}, u32[]{:S(2)}) %collective-permute-start.13) | collective-permute-done | bytes 16416 | tf_op jit(solution)/shard_map/ppermute | solution.py:32
  66.7 0.0 collective-permute-done.12.refs_2_
  66.7 1.1 %shard_map.104 = (bf16[128,2048]{1,0:T(8,128)(2,1)}, f32[4,2048]{1,0:T(4,128)}) custom-call(f32[8,128]{1,0:T(8,128)S(1)} %shard_map.95.meta_ref.refs_0_, f32[128,2048]{1,0:T(8,128)S(1)} %get-tuple-element.19.base_ref, bf16[72,896]{1,0:T(8,128)(2,1)S(1)} %collective-permute-done.10.refs_0_, f32[4,2048]{1,0:T(4,128)S(1)} %get-tuple-element.25.refs_1_, ...), custom_call_target="tpu_custom_call" | custom-call | flops 37748736 | bytes 1867776 | tf_op jit(solution)/shard_map/pallas_call | solution.py:338
  (18 shorter events, 0.0 us)
Async XLA Ops:
  0.6 16.5 %copy-start.6 = (bf16[1,1,288,896]{3,2,1,0:T(8,128)(2,1)S(1)}, bf16[1,1,288,896]{3,2,1,0:T(8,128)(2,1)}, u32[]{:S(2)}) copy-start(bf16[1,1,288,896]{3,2,1,0:T(8,128)(2,1)} %param.15) | copy-start | bytes 1548292
  0.6 9.7 %collective-permute-start = (bf16[128,2048]{1,0:T(8,128)(2,1)}, bf16[128,2048]{1,0:T(8,128)(2,1)S(1)}, u32[]{:S(2)}, u32[]{:S(2)}) collective-permute-start(bf16[128,2048]{1,0:T(8,128)(2,1)} %bitcast.40), channel_id=1, source_target_pairs={{0,24},{8,0},{16,8},{24,16},{1,25},{9,1},{17,9},{25,17},{2,26},{10... | collective-permute-start | bytes 1572872 | tf_op jit(solution)/shard_map/ppermute | solution.py:243
  4.1 17.5 %collective-permute-start.2 = (bf16[128,1280]{1,0:T(8,128)(2,1)S(1)}, bf16[128,1280]{1,0:T(8,128)(2,1)S(1)}, u32[]{:S(2)}, u32[]{:S(2)}) collective-permute-start(bf16[128,1280]{1,0:T(8,128)(2,1)S(1)} %slice_bitcast_fusion), channel_id=1, source_target_pairs={{0,28},{2,30},{4,24},{6,26},{8,4},{10,6},{12,0},{14,2},{16,12},{18... | collective-permute-start | bytes 983048 | tf_op jit(solution)/shard_map/ppermute | solution.py:234
  6.8 1.0 %copy-start.7 = (bf16[1,128,2048]{2,1,0:T(8,128)(2,1)S(1)}, bf16[1,128,2048]{2,1,0:T(8,128)(2,1)}, u32[]{:S(2)}) copy-start(bf16[1,128,2048]{2,1,0:T(8,128)(2,1)} %param.9) | copy-start | bytes 1572868
  7.9 0.7 %copy-start.9 = (bf16[1,2048,4]{1,2,0:T(4,128)(2,1)S(1)}, bf16[1,2048,4]{1,2,0:T(4,128)(2,1)}, u32[]{:S(2)}) copy-start(bf16[1,2048,4]{1,2,0:T(4,128)(2,1)} %param.11) | copy-start | bytes 49156
  8.6 0.7 %copy-start.11 = (s32[1,128,2]{1,2,0:T(2,128)S(1)}, s32[1,128,2]{1,2,0:T(2,128)}, u32[]{:S(2)}) copy-start(s32[1,128,2]{1,2,0:T(2,128)} %param.10) | copy-start | bytes 3076
  10.7 22.6 %collective-permute-start.4 = (bf16[72,2048]{1,0:T(8,128)(2,1)S(1)}, bf16[72,2048]{1,0:T(8,128)(2,1)S(1)}, u32[]{:S(2)}, u32[]{:S(2)}) collective-permute-start(bf16[72,2048]{1,0:T(8,128)(2,1)S(1)} %get-tuple-element.16), channel_id=1, source_target_pairs={{0,2},{2,0},{4,6},{6,4},{1,3},{3,1},{5,7},{7,5},{8,10},{10,8},{12,... | collective-permute-start | bytes 884744 | tf_op jit(solution)/shard_map/ppermute | solution.py:32
  14.2 13.9 %collective-permute-start.3 = (bf16[72,768]{1,0:T(8,128)(2,1)S(1)}, bf16[72,768]{1,0:T(8,128)(2,1)S(1)}, u32[]{:S(2)}, u32[]{:S(2)}) collective-permute-start(bf16[72,768]{1,0:T(8,128)(2,1)S(1)} %get-tuple-element.13), channel_id=1, source_target_pairs={{0,4},{2,6},{4,0},{6,2},{1,5},{3,7},{5,1},{7,3},{8,12},{10,14},{12... | collective-permute-start | bytes 331784 | tf_op jit(solution)/shard_map/ppermute | solution.py:32
  15.3 10.6 %collective-permute-start.1 = (f32[8,128]{1,0:T(8,128)S(1)}, f32[8,128]{1,0:T(8,128)S(1)}, u32[]{:S(2)}, u32[]{:S(2)}) collective-permute-start(f32[8,128]{1,0:T(8,128)S(1)} %shard_map.95.meta_ref.refs_0_), channel_id=1, source_target_pairs={{0,4},{2,6},{4,0},{6,2},{1,5},{3,7},{5,1},{7,3},{8,12},{10,14},{12... | collective-permute-start | bytes 12296 | tf_op jit(solution)/shard_map/ppermute | solution.py:32
  17.2 1.5 %copy-start = (bf16[1,1,448,2048]{3,2,1,0:T(8,128)(2,1)S(1)}, bf16[1,1,448,2048]{3,2,1,0:T(8,128)(2,1)}, u32[]{:S(2)}) copy-start(bf16[1,1,448,2048]{3,2,1,0:T(8,128)(2,1)} %param.12) | copy-start | bytes 5505028
  18.7 1.5 %copy-start.2 = (bf16[1,1,448,2048]{3,2,1,0:T(8,128)(2,1)S(1)}, bf16[1,1,448,2048]{3,2,1,0:T(8,128)(2,1)}, u32[]{:S(2)}) copy-start(bf16[1,1,448,2048]{3,2,1,0:T(8,128)(2,1)} %param.13) | copy-start | bytes 5505028
  20.2 1.5 %copy-start.4 = (bf16[1,1,448,2048]{3,2,1,0:T(8,128)(2,1)S(1)}, bf16[1,1,448,2048]{3,2,1,0:T(8,128)(2,1)}, u32[]{:S(2)}) copy-start(bf16[1,1,448,2048]{3,2,1,0:T(8,128)(2,1)} %param.14) | copy-start | bytes 5505028
  21.7 6.5 %copy-start.1 = (bf16[1,1,448,2048]{3,2,1,0:T(8,128)(2,1)S(1)}, bf16[1,1,448,2048]{3,2,1,0:T(8,128)(2,1)}, u32[]{:S(2)}) copy-start(bf16[1,1,448,2048]{3,2,1,0:T(8,128)(2,1)} %param.12) | copy-start | bytes 5505028
  21.9 13.2 %collective-permute-start.8 = (bf16[72,768]{1,0:T(8,128)(2,1)S(1)}, bf16[72,768]{1,0:T(8,128)(2,1)S(1)}, u32[]{:S(2)}, u32[]{:S(2)}) collective-permute-start(bf16[72,768]{1,0:T(8,128)(2,1)S(1)} %shard_map.101), channel_id=1, source_target_pairs={{0,6},{2,4},{4,2},{6,0},{1,7},{3,5},{5,3},{7,1},{8,14},{10,12},{12... | collective-permute-start | bytes 331784 | tf_op jit(solution)/shard_map/ppermute | solution.py:32
  26.1 7.3 %copy-start.3 = (bf16[1,1,448,2048]{3,2,1,0:T(8,128)(2,1)S(1)}, bf16[1,1,448,2048]{3,2,1,0:T(8,128)(2,1)}, u32[]{:S(2)}) copy-start(bf16[1,1,448,2048]{3,2,1,0:T(8,128)(2,1)} %param.13) | copy-start | bytes 5505028
  26.1 7.3 %copy-start.5 = (bf16[1,1,448,2048]{3,2,1,0:T(8,128)(2,1)S(1)}, bf16[1,1,448,2048]{3,2,1,0:T(8,128)(2,1)}, u32[]{:S(2)}) copy-start(bf16[1,1,448,2048]{3,2,1,0:T(8,128)(2,1)} %param.14) | copy-start | bytes 5505028
  26.1 12.1 %collective-permute-start.7 = (bf16[72,1280]{1,0:T(8,128)(2,1)S(1)}, bf16[72,1280]{1,0:T(8,128)(2,1)S(1)}, u32[]{:S(2)}, u32[]{:S(2)}) collective-permute-start(bf16[72,1280]{1,0:T(8,128)(2,1)S(1)} %shard_map.100), channel_id=1, source_target_pairs={{0,2},{2,0},{4,6},{6,4},{1,3},{3,1},{5,7},{7,5},{8,10},{10,8},{12,... | collective-permute-start | bytes 552968 | tf_op jit(solution)/shard_map/ppermute | solution.py:32
  29.9 18.5 %collective-permute-start.6 = (bf16[72,2176]{1,0:T(8,128)(2,1)S(1)}, bf16[72,2176]{1,0:T(8,128)(2,1)S(1)}, u32[]{:S(2)}, u32[]{:S(2)}) collective-permute-start(bf16[72,2176]{1,0:T(8,128)(2,1)S(1)} %get-tuple-element.17), channel_id=1, source_target_pairs={{0,4},{2,6},{4,0},{6,2},{1,5},{3,7},{5,1},{7,3},{8,12},{10,14},{12... | collective-permute-start | bytes 940040 | tf_op jit(solution)/shard_map/ppermute | solution.py:32
  34.9 19.2 %copy-start.8 = (bf16[1,128,2048]{2,1,0:T(8,128)(2,1)S(1)}, bf16[1,128,2048]{2,1,0:T(8,128)(2,1)}, u32[]{:S(2)}) copy-start(bf16[1,128,2048]{2,1,0:T(8,128)(2,1)} %param.9) | copy-start | bytes 1572868
  35.0 19.2 %copy-start.10 = (bf16[1,2048,4]{1,2,0:T(4,128)(2,1)S(1)}, bf16[1,2048,4]{1,2,0:T(4,128)(2,1)}, u32[]{:S(2)}) copy-start(bf16[1,2048,4]{1,2,0:T(4,128)(2,1)} %param.11) | copy-start | bytes 49156
  35.0 19.2 %collective-permute-start.5 = (bf16[72,2064]{1,0:T(8,128)(2,1)S(1)}, bf16[72,2064]{1,0:T(8,128)(2,1)S(1)}, u32[]{:S(2)}, u32[]{:S(2)}) collective-permute-start(bf16[72,2064]{1,0:T(8,128)(2,1)S(1)} %shard_map.98._), channel_id=1, source_target_pairs={{0,2},{2,0},{4,6},{6,4},{1,3},{3,1},{5,7},{7,5},{8,10},{10,8},{12,... | collective-permute-start | bytes 891656 | tf_op jit(solution)/shard_map/ppermute | solution.py:32
  39.8 13.6 %collective-permute-start.9 = (bf16[72,1280]{1,0:T(8,128)(2,1)S(1)}, bf16[72,1280]{1,0:T(8,128)(2,1)S(1)}, u32[]{:S(2)}, u32[]{:S(2)}) collective-permute-start(bf16[72,1280]{1,0:T(8,128)(2,1)S(1)} %get-tuple-element.18), channel_id=1, source_target_pairs={{0,6},{2,4},{4,2},{6,0},{1,7},{3,5},{5,3},{7,1},{8,14},{10,12},{12... | collective-permute-start | bytes 552968 | tf_op jit(solution)/shard_map/ppermute | solution.py:32
  55.1 4.2 %collective-permute-start.11 = (f32[4,2048]{1,0:T(4,128)S(1)}, f32[4,2048]{1,0:T(4,128)S(1)}, u32[]{:S(2)}, u32[]{:S(2)}) collective-permute-start(f32[4,2048]{1,0:T(4,128)S(1)} %get-tuple-element.21), channel_id=1, source_target_pairs={{0,1},{1,0},{2,3},{3,2},{4,5},{5,4},{6,7},{7,6},{8,9},{9,8},{10,11... | collective-permute-start | bytes 98312 | tf_op jit(solution)/shard_map/ppermute | solution.py:32
  56.7 7.1 %collective-permute-start.10 = (bf16[72,896]{1,0:T(8,128)(2,1)S(1)}, bf16[72,896]{1,0:T(8,128)(2,1)S(1)}, u32[]{:S(2)}, u32[]{:S(2)}) collective-permute-start(bf16[72,896]{1,0:T(8,128)(2,1)S(1)} %get-tuple-element.20), channel_id=1, source_target_pairs={{0,6},{2,4},{4,2},{6,0},{1,7},{3,5},{5,3},{7,1},{8,14},{10,12},{12... | collective-permute-start | bytes 387080 | tf_op jit(solution)/shard_map/ppermute | solution.py:32
  59.3 5.6 %collective-permute-start.14 = (bf16[4,2048]{1,0:T(4,128)(2,1)S(1)}, bf16[4,2048]{1,0:T(4,128)(2,1)S(1)}, u32[]{:S(2)}, u32[]{:S(2)}) collective-permute-start(bf16[4,2048]{1,0:T(4,128)(2,1)S(1)} %get-tuple-element.24), channel_id=1, source_target_pairs={{0,6},{2,4},{4,2},{6,0},{1,7},{3,5},{5,3},{7,1},{8,14},{10,12},{12... | collective-permute-start | bytes 49160 | tf_op jit(solution)/shard_map/ppermute | solution.py:32
  61.9 4.8 %collective-permute-start.13 = (bf16[4,2048]{1,0:T(4,128)(2,1)S(1)}, bf16[4,2048]{1,0:T(4,128)(2,1)S(1)}, u32[]{:S(2)}, u32[]{:S(2)}) collective-permute-start(bf16[4,2048]{1,0:T(4,128)(2,1)S(1)} %get-tuple-element.24), channel_id=1, source_target_pairs={{0,4},{2,6},{4,0},{6,2},{1,5},{3,7},{5,1},{7,3},{8,12},{10,14},{12... | collective-permute-start | bytes 49160 | tf_op jit(solution)/shard_map/ppermute | solution.py:32
  62.4 4.3 %collective-permute-start.12 = (bf16[4,2048]{1,0:T(4,128)(2,1)S(1)}, bf16[4,2048]{1,0:T(4,128)(2,1)S(1)}, u32[]{:S(2)}, u32[]{:S(2)}) collective-permute-start(bf16[4,2048]{1,0:T(4,128)(2,1)S(1)} %get-tuple-element.24), channel_id=1, source_target_pairs={{0,2},{2,0},{4,6},{6,4},{1,3},{3,1},{5,7},{7,5},{8,10},{10,8},{12,... | collective-permute-start | bytes 49160 | tf_op jit(solution)/shard_map/ppermute | solution.py:32
